TPU v7x, 512 devices: a whole 4x8x8 slice. The times are simulated.
512 devices in a mesh: ctx: 64 (over z_hi, y, core), kv: 8 (over x, z_lo).
Axes of the slice: x: 4, y: 8, z: 8 (z_hi: 4, z_lo: 2; z = z_hi * 2 + z_lo), core: 2. Of those that a mesh axis runs over, the one named last changes fastest.
Arguments:
- query: bfloat16 [24576, 4096], P('ctx', 'kv'), may hold values from -9 to 9
- keys: bfloat16 [24576, 1024], P('ctx', 'kv'), may hold values from -8.4 to 8.4
- values: bfloat16 [24576, 1024], P('ctx', 'kv'), may hold values from -6 to 6
- vertical: int32 [8, 16], P('kv'), may hold values from 0 to 383, as said below
- slash: int32 [8, 768], P('kv'), may hold values from 0 to 2048, as said below
- out_weight: bfloat16 [4096, 4096], P('kv', 'ctx'), may hold values from -0.5 to 0.5
Outputs:
- projected: bfloat16 [24576, 4096], P(('ctx', 'kv'))
Inputs may be any that keep to these rules, and one draw needn't show every extreme that they name: `vertical`: the 16 blocks of one KV head are distinct, and every KV head lists block 0. `slash`: the 768 offsets of one KV head are distinct, and every KV head lists offset 0.
All inputs are finite; a program needn't handle non-finite values.
Results may differ from a plain program's by a relative error of at most 0.017.
Values may be sent and summed in bfloat16 or wider, within the bound.
No kernel may reach another device: no remote copies, remote signals or barrier semaphores. Data moves between devices by JAX's collectives and lax.ppermute only.
A program may use at most 64 MiB of HBM per device.

v0:
```python
import math

import jax
import jax.numpy as jnp
from jax import lax
from jax.sharding import PartitionSpec as P

BLK = 64
SLASH_MAX = 2048


def shifted(shard, axis, by):
    peers = lax.axis_size(axis)
    pairs = [(i, i + by) for i in range(peers) if 0 <= i + by < peers]
    return lax.ppermute(shard, axis, pairs)


def body(query, keys, values, vertical, slash, out_weight):
    rows = keys.shape[0]
    width = keys.shape[1]
    group = query.shape[1] // width
    n_ctx = lax.axis_size("ctx")
    place = lax.axis_index("ctx")
    listed = vertical[0]
    offsets = slash[0]
    listed_rows = listed.shape[0] * BLK
    per_shard = rows // BLK
    local_ids = listed - place * per_shard
    picker = (local_ids[:, None] == jnp.arange(per_shard, dtype=jnp.int32)[None, :]).astype(
        jnp.bfloat16
    )
    key_pick = jnp.dot(
        picker, keys.reshape(per_shard, BLK * width), preferred_element_type=jnp.float32
    )
    value_pick = jnp.dot(
        picker, values.reshape(per_shard, BLK * width), preferred_element_type=jnp.float32
    )
    key_pick = key_pick.reshape(listed_rows, width)
    value_pick = value_pick.reshape(listed_rows, width)
    far_keys, far_values = lax.psum((key_pick, value_pick), "ctx")
    far_keys = far_keys.astype(jnp.bfloat16)
    far_values = far_values.astype(jnp.bfloat16)
    paired = jnp.stack([keys, values])
    reach = min(-(-SLASH_MAX // rows), n_ctx - 1)
    pad_rows = max(0, SLASH_MAX - reach * rows)
    pieces = [shifted(paired, "ctx", step) for step in range(reach, 0, -1)]
    band = jnp.concatenate(pieces + [paired], axis=1)
    base_row = pad_rows + reach * rows
    band = band[:, base_row - SLASH_MAX :]
    q_block = min(rows, 128)
    n_steps = rows // q_block
    span = SLASH_MAX + q_block
    cycle = SLASH_MAX + 2 * q_block
    slash_flags = jnp.zeros((SLASH_MAX + 1,), jnp.bool_).at[offsets].set(True)
    pattern = jnp.concatenate([slash_flags[::-1], jnp.zeros((cycle - SLASH_MAX - 1,), jnp.bool_)])
    diagonal_ok = jnp.tile(pattern, q_block)[: q_block * (cycle - 1)].reshape(q_block, cycle - 1)[
        :, :span
    ]
    n_blocks = n_ctx * rows // BLK
    block_flags = jnp.zeros((n_blocks,), jnp.bool_).at[listed].set(True)
    far_pos = (listed[:, None] * BLK + jnp.arange(BLK, dtype=jnp.int32)[None, :]).reshape(-1)
    queries = query.reshape(rows, group, width)
    scale = 1.0 / math.sqrt(width)

    def attend(step_id):
        first = step_id * q_block
        q_rows = lax.dynamic_slice_in_dim(queries, first, q_block, 0)
        window = lax.dynamic_slice_in_dim(band, first, span, 1)
        q_pos = place * rows + first + jnp.arange(q_block, dtype=jnp.int32)
        k_pos = place * rows + first - SLASH_MAX + jnp.arange(span, dtype=jnp.int32)
        listed_col = jnp.take(block_flags, jnp.clip(k_pos // BLK, 0, n_blocks - 1))
        column_ok = (k_pos >= 0) & jnp.logical_not(listed_col)
        band_ok = diagonal_ok & column_ok[None, :]
        far_scores = (
            jnp.einsum("tgd,kd->gtk", q_rows, far_keys, preferred_element_type=jnp.float32) * scale
        )
        far_ok = far_pos[None, :] <= q_pos[:, None]
        far_scores = jnp.where(far_ok[None], far_scores, -1e30)
        band_scores = (
            jnp.einsum("tgd,kd->gtk", q_rows, window[0], preferred_element_type=jnp.float32) * scale
        )
        band_scores = jnp.where(band_ok[None], band_scores, -1e30)
        top = jnp.maximum(jnp.max(far_scores, axis=-1), jnp.max(band_scores, axis=-1))
        far_weights = jnp.exp(far_scores - top[:, :, None])
        band_weights = jnp.exp(band_scores - top[:, :, None])
        total = jnp.sum(far_weights, axis=-1) + jnp.sum(band_weights, axis=-1)
        mixed = jnp.einsum(
            "gtk,kd->tgd",
            far_weights.astype(jnp.bfloat16),
            far_values,
            preferred_element_type=jnp.float32,
        )
        mixed = mixed + jnp.einsum(
            "gtk,kd->tgd",
            band_weights.astype(jnp.bfloat16),
            window[1],
            preferred_element_type=jnp.float32,
        )
        return (mixed / total.T[:, :, None]).astype(jnp.bfloat16).reshape(q_block, group * width)

    attended = lax.map(attend, jnp.arange(n_steps, dtype=jnp.int32)).reshape(rows, group * width)
    partial_sum = jnp.dot(
        attended,
        lax.all_gather(out_weight, "ctx", axis=1, tiled=True),
        preferred_element_type=jnp.float32,
    )
    rounded = lax.optimization_barrier(partial_sum.astype(jnp.bfloat16)).astype(jnp.float32)
    summed = lax.psum_scatter(rounded.astype(jnp.bfloat16), "kv", scatter_dimension=0, tiled=True)
    return summed


def solution(mesh):
    return jax.shard_map(
        body,
        mesh=mesh,
        in_specs=(
            P("ctx", "kv"),
            P("ctx", "kv"),
            P("ctx", "kv"),
            P("kv", None),
            P("kv", None),
            P("kv", "ctx"),
        ),
        out_specs=P(("ctx", "kv"), None),
        check_vma=False,
    )
```

profile of v0, /device:TPU:1, one launch (start us, length us, event | category | flops | bytes accessed | tf_op | source)
XLA Modules:
  0.0 550.7 jit_solution(5927784807895069642)
XLA Ops:
  7.5 6.1 %collective-permute-start = (bf16[2,384,128]{2,1,0:T(8,128)(2,1)S(1)}, bf16[2,384,128]{2,1,0:T(8,128)(2,1)S(1)}, u32[]{:S(2)}, u32[]{:S(2)}) collective-permute-start(bf16[2,384,128]{2,1,0:T(8,128)(2,1)S(1)} %pad_maximum_fusion), channel_id=1, source_target_pairs={{0,48},{8,56},{16,64},{24,72},{32,80},{40,88},{48,96},{56,104},{64... | collective-permute-start | bytes 589832 | tf_op jit(solution)/shard_map/ppermute | solution.py:15
  13.6 5.5 collective-permute-start.1
  19.1 5.1 collective-permute-start.2
  24.2 2.9 collective-permute-start.3
  27.1 3.2 collective-permute-start.4
  34.1 293.4 %all-reduce.3 = (bf16[1024,128]{1,0:T(8,128)(2,1)}, bf16[1024,128]{0,1:T(8,128)(2,1)}) all-reduce(f32[1024,128]{1,0:T(8,128)S(1)} %reshape.268, f32[1024,128]{0,1:T(8,128)S(1)} %copy.13), channel_id=1, replica_groups=mesh['ctx'=64,'kv'=8] {'ctx'}, use_global_device_ids=true, to_apply=%region_2.0 | all-reduce | flops 262144 | bytes 1572864 | tf_op jit(solution)/shard_map/psum | solution.py:40
  327.6 3.4 scatter_custom_fusion.1
  335.8 3.5 collective-permute-start.5
  339.5 4.9 collective-permute-done.5
  344.6 94.5 %while.13 = (s32[]{:T(128)}, bf16[3,128,512]{2,1,0:T(8,128)(2,1)}, s32[3]{0:T(128)S(1)}, s32[]{:T(128)}, bf16[384,4,128]{0,2,1:T(8,128)(2,1)}, /*index=5*/bf16[1...) while((s32[]{:T(128)}, bf16[3,128,512]{2,1,0:T(8,128)(2,1)}, ...), condition=%wide.region_9.10_spmd.clone, body=%wide.region_4.9_spmd.clone.sunk | while | flops 853138432 | bytes 25247768 | solution.py:101
  346.1 12.6 %gather_fusion = pred[2176]{0:T(1024)(128)(4,1)S(1)} fusion(pred[384]{0:T(512)(128)(4,1)S(1)} %get-tuple-element.330, s32[3072]{0:T(1024)S(1)} %pad_clamp_fusion.2), kind=kCustom, calls=%fused_computation.clone.clone.1 | custom fusion | bytes 13056 | tf_op jit(solution)/shard_map/while/body/eval_jaxpr/jit(_take)/gather | solution.py:71
  360.8 3.7 fusion.69
  366.4 2.9 fusion.72
  369.9 3.2 fusion.70
  377.6 12.6 %gather_fusion = pred[2176]{0:T(1024)(128)(4,1)S(1)} fusion(pred[384]{0:T(512)(128)(4,1)S(1)} %get-tuple-element.330, s32[3072]{0:T(1024)S(1)} %pad_clamp_fusion.2), kind=kCustom, calls=%fused_computation.clone.clone.1 | custom fusion | bytes 13056 | tf_op jit(solution)/shard_map/while/body/eval_jaxpr/jit(_take)/gather | solution.py:71
  392.3 3.7 fusion.69
  397.9 2.9 fusion.72
  401.4 3.2 fusion.70
  409.1 12.6 %gather_fusion = pred[2176]{0:T(1024)(128)(4,1)S(1)} fusion(pred[384]{0:T(512)(128)(4,1)S(1)} %get-tuple-element.330, s32[3072]{0:T(1024)S(1)} %pad_clamp_fusion.2), kind=kCustom, calls=%fused_computation.clone.clone.1 | custom fusion | bytes 13056 | tf_op jit(solution)/shard_map/while/body/eval_jaxpr/jit(_take)/gather | solution.py:71
  423.8 3.7 fusion.69
  429.4 2.9 fusion.72
  432.9 3.2 fusion.70
  439.2 5.8 %convolution_convert_fusion = bf16[384,4096]{1,0:T(8,128)(2,1)} fusion(bf16[384,512]{1,0:T(8,128)(2,1)} %bitcast.98, bf16[512,4096]{0,1:T(8,128)(2,1)} %all-gather.2.cloned.1.call-done), kind=kOutput, calls=%fused_computation.64 | convolution fusion | flops 1612185600 | bytes 7733248 | tf_op jit(solution)/shard_map/dot_general | solution.py:102
  445.0 98.8 %reduce-scatter.2.cloned.1.call-done = bf16[48,4096]{1,0:T(8,128)(2,1)} async-done(((bf16[384,4096]{1,0:T(8,128)(2,1)}), bf16[48,4096]{1,0:T(8,128)(2,1)}) %reduce-scatter.2.cloned.1.call-update) | async-done | bytes 393232 | tf_op jit(solution)/shard_map/reduce_scatter | solution.py:108
  (107 shorter events, 34.9 us)
Async XLA Ops:
  6.5 432.6 %all-gather.2.cloned.1.call-start = ((), (), s32[]{:S(2)}) async-start(), calls=%async_computation.1 | async-start | bytes 4259840 | tf_op jit(solution)/shard_map/all_gather | solution.py:104
  7.5 328.3 %collective-permute-start = (bf16[2,384,128]{2,1,0:T(8,128)(2,1)S(1)}, bf16[2,384,128]{2,1,0:T(8,128)(2,1)S(1)}, u32[]{:S(2)}, u32[]{:S(2)}) collective-permute-start(bf16[2,384,128]{2,1,0:T(8,128)(2,1)S(1)} %pad_maximum_fusion), channel_id=1, source_target_pairs={{0,48},{8,56},{16,64},{24,72},{32,80},{40,88},{48,96},{56,104},{64... | collective-permute-start | bytes 589832 | tf_op jit(solution)/shard_map/ppermute | solution.py:15
  13.6 325.7 %collective-permute-start.1 = (bf16[2,384,128]{2,1,0:T(8,128)(2,1)S(1)}, bf16[2,384,128]{2,1,0:T(8,128)(2,1)S(1)}, u32[]{:S(2)}, u32[]{:S(2)}) collective-permute-start(bf16[2,384,128]{2,1,0:T(8,128)(2,1)S(1)} %pad_maximum_fusion), channel_id=1, source_target_pairs={{0,40},{8,48},{16,56},{24,64},{32,72},{40,80},{48,88},{56,96},{64,... | collective-permute-start | bytes 589832 | tf_op jit(solution)/shard_map/ppermute | solution.py:15
  19.1 320.3 %collective-permute-start.2 = (bf16[2,384,128]{2,1,0:T(8,128)(2,1)S(1)}, bf16[2,384,128]{2,1,0:T(8,128)(2,1)S(1)}, u32[]{:S(2)}, u32[]{:S(2)}) collective-permute-start(bf16[2,384,128]{2,1,0:T(8,128)(2,1)S(1)} %pad_maximum_fusion), channel_id=1, source_target_pairs={{0,32},{8,40},{16,48},{24,56},{32,64},{40,72},{48,80},{56,88},{64,... | collective-permute-start | bytes 589832 | tf_op jit(solution)/shard_map/ppermute | solution.py:15
  24.2 315.2 %collective-permute-start.3 = (bf16[2,384,128]{2,1,0:T(8,128)(2,1)S(1)}, bf16[2,384,128]{2,1,0:T(8,128)(2,1)S(1)}, u32[]{:S(2)}, u32[]{:S(2)}) collective-permute-start(bf16[2,384,128]{2,1,0:T(8,128)(2,1)S(1)} %pad_maximum_fusion), channel_id=1, source_target_pairs={{0,24},{8,32},{16,40},{24,48},{32,56},{40,64},{48,72},{56,80},{64,... | collective-permute-start | bytes 589832 | tf_op jit(solution)/shard_map/ppermute | solution.py:15
  27.1 312.3 %collective-permute-start.4 = (bf16[2,384,128]{2,1,0:T(8,128)(2,1)S(1)}, bf16[2,384,128]{2,1,0:T(8,128)(2,1)S(1)}, u32[]{:S(2)}, u32[]{:S(2)}) collective-permute-start(bf16[2,384,128]{2,1,0:T(8,128)(2,1)S(1)} %pad_maximum_fusion), channel_id=1, source_target_pairs={{0,16},{8,24},{16,32},{24,40},{32,48},{40,56},{48,64},{56,72},{64,... | collective-permute-start | bytes 589832 | tf_op jit(solution)/shard_map/ppermute | solution.py:15
  30.4 513.5 %reduce-scatter.2.cloned.1.call-start = ((), (), s32[]{:S(2)}) async-start(), calls=%async_computation.2 | async-start | bytes 3538944 | tf_op jit(solution)/shard_map/reduce_scatter | solution.py:108
  33.5 294.0 %copy-start.4 = (s32[1,16]{1,0:T(1,128)S(1)}, s32[1,16]{1,0:T(1,128)}, u32[]{:S(2)}) copy-start(s32[1,16]{1,0:T(1,128)} %param.11) | copy-start | bytes 196
  33.5 294.0 %copy-start.3 = (s32[1,768]{1,0:T(1,128)S(1)}, s32[1,768]{1,0:T(1,128)}, u32[]{:S(2)}) copy-start(s32[1,768]{1,0:T(1,128)} %param.12) | copy-start | bytes 9220
  34.1 300.1 %copy-start.2 = (bf16[384,512]{1,0:T(8,128)(2,1)S(1)}, bf16[384,512]{1,0:T(8,128)(2,1)}, u32[]{:S(2)}) copy-start(bf16[384,512]{1,0:T(8,128)(2,1)} %param.8) | copy-start | bytes 1179652
  333.0 11.5 %copy-start = (bf16[384,128]{1,0:T(8,128)(2,1)S(1)}, bf16[384,128]{1,0:T(8,128)(2,1)}, u32[]{:S(2)}) copy-start(bf16[384,128]{1,0:T(8,128)(2,1)} %param.9) | copy-start | bytes 294916
  333.0 11.5 %copy-start.1 = (bf16[384,128]{1,0:T(8,128)(2,1)S(1)}, bf16[384,128]{1,0:T(8,128)(2,1)}, u32[]{:S(2)}) copy-start(bf16[384,128]{1,0:T(8,128)(2,1)} %param.10) | copy-start | bytes 294916
  335.8 8.7 %collective-permute-start.5 = (bf16[2,384,128]{2,1,0:T(8,128)(2,1)S(1)}, bf16[2,384,128]{2,1,0:T(8,128)(2,1)S(1)}, u32[]{:S(2)}, u32[]{:S(2)}) collective-permute-start(bf16[2,384,128]{2,1,0:T(8,128)(2,1)S(1)} %pad_maximum_fusion), channel_id=1, source_target_pairs={{0,8},{8,16},{16,24},{24,32},{32,40},{40,48},{48,56},{56,64},{64,7... | collective-permute-start | bytes 589832 | tf_op jit(solution)/shard_map/ppermute | solution.py:15
  369.9 3.2 copy-start.5
  401.4 3.2 copy-start.5
  432.9 3.2 copy-start.5
Sparse Core Ops, SparseCore 0:
  30.5 108.0 all-gather.1
  445.1 98.6 reduce-scatter.1
where the time goes:
time: 551 us
  blocking collectives  293 us (53%)
  waiting for transfers between devices  104 us (19%)
  local copies, waits for them, and re-layouts  55.7 us (10%)
  matrix products  35.9 us (7%)
  starting transfers between devices  26.3 us (5%)
  other arithmetic  19.3 us (4%)
  between operations  13.7 us (2%)
    psum x1, blocking collectives, body(): far_keys, far_values = lax.psum((key_pick, value_pick), 'ctx')  293 us
    reduce_scatter x1, waiting for transfers between devices, body(): lax.psum_scatter(rounded.astype(jnp.bfloat16), 'kv', scatter_dimension=0,...  98.8 us
    gather x3, local copies, waits for them, and re-layouts, attend(): listed_col = jnp.take(block_flags, jnp.clip(k_pos // BLK, 0, n_blocks - 1))  37.7 us
    ppermute x6, starting transfers between devices, shifted(): return lax.ppermute(shard, axis, pairs)  26.3 us
  transfers between devices with their start and end apart: 8, of which 2 were waited for; matrix products, arithmetic and copies ran while one was open for 19% of the time, Pallas kernels for 0%

commit v1 on v0

v1 whole, which is shorter than its diff:
```python
import functools
import math

import jax
import jax.numpy as jnp
from jax import lax
from jax.experimental import pallas as pl
from jax.experimental.pallas import tpu as pltpu
from jax.sharding import Mesh, PartitionSpec as P

BLK = 64
SLASH_MAX = 2048
HD = 128
GROUP = 4
QB = 128
MASKED = -1e30
CTX = ("zh", "y", "c")
KV = ("x", "zl")
SCALE = math.log2(math.e) / math.sqrt(HD)
NT = (((1,), (1,)), ((), ()))
VMEM_LIMIT = 48 * 1024 * 1024


def vmem(n):
    return [pl.BlockSpec(memory_space=pltpu.VMEM)] * n


def pick_kernel(ids_ref, k_ref, v_ref, pair_ref, keep_ref, send_ref):
    rows = k_ref.shape[0]
    pair_ref[0] = k_ref[...]
    pair_ref[1] = v_ref[...]
    half = keep_ref.shape[0]
    for slot in range(2 * half):
        block = ids_ref[slot]
        here = jnp.logical_and(block >= 0, block < rows // BLK)
        row = pl.multiple_of(jnp.clip(block, 0, rows // BLK - 1) * BLK, BLK)
        out = keep_ref if slot < half else send_ref
        for part, ref in enumerate((k_ref, v_ref)):
            got = ref[pl.ds(row, BLK), :].astype(jnp.float32)
            out[slot % half, part] = jnp.where(here, got, 0.0).astype(jnp.bfloat16)


def stacked_queries(q_ref, first):
    return jnp.concatenate(
        [q_ref[pl.ds(first, QB), h * HD : (h + 1) * HD] for h in range(GROUP)], axis=0
    )


def lane_fold(op, x):
    out = x[:, :HD]
    for i in range(1, x.shape[1] // HD):
        out = op(out, x[:, i * HD : (i + 1) * HD])
    return out


def band_kernel(q_ref, line_ref, col_ref, *refs):
    pieces, (acc_ref, top_ref, sum_ref), (diag, bias, kwin, vwin, s_scr) = refs[:7], refs[7:10], refs[10:]
    rows = q_ref.shape[0]
    span = SLASH_MAX + QB
    lead = 7 * rows - rows - SLASH_MAX
    for i, piece in enumerate(pieces):
        kwin[i * rows : (i + 1) * rows] = piece[0]
        vwin[i * rows : (i + 1) * rows] = piece[1]
    diag[...] = pltpu.roll(
        jnp.broadcast_to(line_ref[...], (QB, span)), 0, 1, stride=1, stride_axis=0
    )
    chunks = [(at, min(256, span - at)) for at in range(0, span, 256)]

    @pl.loop(0, rows // QB)
    def _(step):
        first = pl.multiple_of(step * QB, QB)
        base = pl.multiple_of(lead + step * QB, QB)
        bias[...] = diag[...] + col_ref[:, pl.ds(base, span)]
        q = stacked_queries(q_ref, first)
        top = jnp.full((GROUP * QB, HD), MASKED, jnp.float32)
        for at, width in chunks:
            k = kwin[pl.ds(base + at, width), :]
            s = lax.dot_general(q, k, NT, preferred_element_type=jnp.float32)
            b = bias[:, at : at + width]
            s = s + jnp.concatenate([b] * GROUP, axis=0)
            s_scr[:, at : at + width] = s
            top = jnp.maximum(top, lane_fold(jnp.maximum, s))
        top = jnp.max(top, axis=1, keepdims=True)
        shift = top * SCALE
        acc = jnp.zeros((GROUP * QB, HD), jnp.float32)
        total = jnp.zeros((GROUP * QB, HD), jnp.float32)
        for at, width in chunks:
            p = jnp.exp2(s_scr[:, at : at + width] * SCALE - shift)
            total = total + lane_fold(jnp.add, p)
            v = vwin[pl.ds(base + at, width), :]
            acc = acc + jnp.dot(p.astype(jnp.bfloat16), v, preferred_element_type=jnp.float32)
        acc_ref[step] = acc
        sum_ref[step] = total
        top_ref[step] = jnp.broadcast_to(top, (GROUP * QB, HD))


def far_kernel(place_ref, q_ref, pos_ref, mine_ref, other_ref, acc_ref, top_ref, sum_ref,
               w_mine, w_other, out_ref, w_scr, kfar, vfar, attended, sems):
    rows = q_ref.shape[0]
    core = place_ref[1]
    n_y, n_zh = w_mine.shape[0], w_mine.shape[1]
    copies = []
    for i, (src, at) in enumerate(((w_mine, core), (w_other, 1 - core))):
        for z in range(n_zh):
            copy = pltpu.make_async_copy(
                src.at[:, z], w_scr.at[pl.ds(z * n_y, n_y), at], sems.at[i * n_zh + z]
            )
            copy.start()
            copies.append(copy)
    half = mine_ref.shape[0]
    for i in range(half):
        for j, ref in enumerate((mine_ref, other_ref)):
            at = (j * half + i) * BLK
            kfar[at : at + BLK] = ref[i, 0]
            vfar[at : at + BLK] = ref[i, 1]
    n_far = kfar.shape[0]
    chunks = [(at, 256) for at in range(0, n_far, 256)]

    @pl.loop(0, rows // QB)
    def _(step):
        first = pl.multiple_of(step * QB, QB)
        q = stacked_queries(q_ref, first)
        q_pos = place_ref[0] * rows + first + lax.broadcasted_iota(jnp.int32, (QB, 256), 0)
        band_top = top_ref[step]
        top = band_top
        scores = []
        for at, width in chunks:
            s = lax.dot_general(q, kfar[at : at + width], NT, preferred_element_type=jnp.float32)
            ok = pos_ref[:, at : at + width] <= q_pos
            b = jnp.where(ok, 0.0, MASKED)
            s = s + jnp.concatenate([b] * GROUP, axis=0)
            scores.append(s)
            top = jnp.maximum(top, lane_fold(jnp.maximum, s))
        top = jnp.max(top, axis=1, keepdims=True)
        shift = top * SCALE
        fade = jnp.exp2(band_top * SCALE - shift)
        acc = acc_ref[step] * fade
        total = sum_ref[step] * fade
        for (at, width), s in zip(chunks, scores):
            p = jnp.exp2(s * SCALE - shift)
            total = total + lane_fold(jnp.add, p)
            acc = acc + jnp.dot(
                p.astype(jnp.bfloat16), vfar[at : at + width], preferred_element_type=jnp.float32
            )
        out = (acc / jnp.sum(total, axis=1, keepdims=True)).astype(jnp.bfloat16)
        for h in range(GROUP):
            attended[pl.ds(first, QB), h * HD : (h + 1) * HD] = out[h * QB : (h + 1) * QB]

    for copy in copies:
        copy.wait()
    width = 512
    per = width // w_scr.shape[2] // 2

    @pl.loop(0, out_ref.shape[1] // width)
    def _(n):
        w = w_scr[pl.ds(n * per, per)].reshape(width, GROUP * HD)
        at = pl.multiple_of(n * width, width)
        out_ref[:, pl.ds(at, width)] = lax.dot_general(
            attended[...], w, NT, preferred_element_type=jnp.float32
        ).astype(jnp.bfloat16)


def swap(x):
    return lax.ppermute(x, "c", [(0, 1), (1, 0)])


def spread(x, axis):
    n = lax.axis_size(axis)
    return lax.all_to_all(jnp.broadcast_to(x[None], (n,) + x.shape), axis, 0, 0, tiled=True)


def summed(x):
    return jnp.sum(x.astype(jnp.float32), axis=0).astype(jnp.bfloat16)


def body(query, keys, values, vertical, slash, out_weight):
    rows, width = keys.shape
    n_ctx = lax.axis_size(CTX)
    place = lax.axis_index(CTX)
    core = lax.axis_index("c")
    listed = vertical[0]
    offsets = slash[0]
    n_listed = listed.shape[0]
    half = n_listed // 2
    per_shard = rows // BLK
    span = SLASH_MAX + QB
    bf16, f32 = jnp.bfloat16, jnp.float32

    ordered = jnp.where(core == 0, listed, jnp.roll(listed, half))
    pair, keep, send = pl.pallas_call(
        pick_kernel,
        in_specs=[pl.BlockSpec(memory_space=pltpu.SMEM)] + vmem(2),
        out_specs=vmem(3),
        out_shape=[
            jax.ShapeDtypeStruct((2, rows, width), bf16),
            jax.ShapeDtypeStruct((half, 2, BLK, width), bf16),
            jax.ShapeDtypeStruct((half, 2, BLK, width), bf16),
        ],
        name="pick",
    )(ordered - place * per_shard, keys, values)

    blocks = keep + swap(send)
    blocks = summed(lax.all_to_all(blocks, "y", 0, 0, tiled=True))
    blocks = summed(spread(blocks, "zh"))
    far_mine = spread(blocks, "y")
    far_other = swap(far_mine)

    ahead = [(i, i + 2) for i in range(n_ctx - 2)]
    own = [pair]
    for _ in range(3):
        own.append(lax.ppermute(own[-1], CTX, ahead))
    other = [swap(jnp.where(core == 0, own[k - 1], own[k])) for k in (1, 2, 3)]
    band = [own[3], other[2], own[2], other[1], own[1], other[0], own[0]]

    w = spread(out_weight.T, "zh")
    w_mine = lax.all_gather(w, "y", axis=0, tiled=False)
    w_other = swap(w_mine)

    distance = SLASH_MAX - jnp.arange(span, dtype=jnp.int32)
    line = jnp.where(jnp.any(distance[None, :] == offsets[:, None], axis=0), 0.0, MASKED)
    k_pos = (place - 6) * rows + jnp.arange(7 * rows, dtype=jnp.int32)
    is_listed = jnp.any((k_pos // BLK)[None, :] == listed[:, None], axis=0)
    column = jnp.where((k_pos >= 0) & jnp.logical_not(is_listed), 0.0, MASKED)
    far_pos = ordered[:, None] * BLK + jnp.arange(BLK, dtype=jnp.int32)[None, :]

    steps = rows // QB
    stats = jax.ShapeDtypeStruct((steps, GROUP * QB, HD), f32)
    acc, top, total = pl.pallas_call(
        band_kernel,
        in_specs=vmem(10),
        out_specs=vmem(3),
        out_shape=[stats, stats, stats],
        scratch_shapes=[
            pltpu.VMEM((QB, span), f32),
            pltpu.VMEM((QB, span), f32),
            pltpu.VMEM((7 * rows, HD), bf16),
            pltpu.VMEM((7 * rows, HD), bf16),
            pltpu.VMEM((GROUP * QB, span), f32),
        ],
        compiler_params=pltpu.CompilerParams(vmem_limit_bytes=VMEM_LIMIT),
        cost_estimate=pl.CostEstimate(
            flops=4 * rows * GROUP * HD * span,
            bytes_accessed=8_000_000,
            transcendentals=rows * GROUP * span,
        ),
        name="band",
    )(query, line[None], column[None], *band)

    n_far = n_listed * BLK
    d_model = out_weight.shape[1] * n_ctx
    partial_sum = pl.pallas_call(
        far_kernel,
        in_specs=[pl.BlockSpec(memory_space=pltpu.SMEM)] + vmem(7)
        + [pl.BlockSpec(memory_space=pl.ANY)] * 2,
        out_specs=pl.BlockSpec(memory_space=pltpu.VMEM),
        out_shape=jax.ShapeDtypeStruct((rows, d_model), bf16),
        scratch_shapes=[
            pltpu.VMEM((n_ctx // 2, 2, out_weight.shape[1], GROUP * HD), bf16),
            pltpu.VMEM((n_far, HD), bf16),
            pltpu.VMEM((n_far, HD), bf16),
            pltpu.VMEM((rows, GROUP * HD), bf16),
            pltpu.SemaphoreType.DMA((2 * lax.axis_size("zh"),)),
        ],
        compiler_params=pltpu.CompilerParams(vmem_limit_bytes=VMEM_LIMIT),
        cost_estimate=pl.CostEstimate(
            flops=4 * rows * GROUP * HD * n_far + 2 * rows * GROUP * HD * d_model,
            bytes_accessed=10_000_000,
            transcendentals=rows * GROUP * n_far,
        ),
        name="far",
    )(
        jnp.stack([place, core]).astype(jnp.int32),
        query,
        far_pos.reshape(1, n_far),
        far_mine,
        far_other,
        acc,
        top,
        total,
        w_mine,
        w_other,
    )
    received = lax.all_to_all(partial_sum.reshape(8, rows // 8, d_model), KV, 0, 0, tiled=True)
    return summed(received)


def solution(mesh):
    fine = Mesh(mesh.devices.reshape(4, 8, 2, 4, 2), CTX + KV)
    return jax.shard_map(
        body,
        mesh=fine,
        in_specs=(
            P(CTX, KV),
            P(CTX, KV),
            P(CTX, KV),
            P(KV, None),
            P(KV, None),
            P(KV, CTX),
        ),
        out_specs=P(CTX + KV, None),
        check_vma=False,
    )
```

time: 551 us -> 216 us (0.39)
  blocking collectives: 293 us -> 61.5 us
  local copies, waits for them, and re-layouts: 55.7 us -> 3.24 us
  waiting for transfers between devices: 104 us -> 53.9 us
  matrix products: 35.9 us -> 0 us
  starting transfers between devices: 26.3 us -> 54.8 us
  Pallas kernels: 0 us -> 20.8 us
  other arithmetic: 19.3 us -> 7.16 us
    psum x1 -> x0, blocking collectives: 293 us -> none  [body(): far_keys, far_values = lax.psum((key_pick, value_pick), 'ctx')]
    reduce_scatter x1 -> x0, waiting for transfers between devices: 98.8 us -> none  [body(): lax.psum_scatter(rounded.astype(jnp.bfloat16), 'kv', scatter_dimension=0,...]
    all_to_all x0 -> x2, blocking collectives: none -> 61.5 us  [the longest x1 42 us: body(): lax.all_to_all(partial_sum.reshape(8, rows // 8, d_model), KV, 0, 0, tile...]
    all_gather x1, waiting for transfers between devices: 0.01 us -> 39.1 us  [body(): w_mine = lax.all_gather(w, 'y', axis=0, tiled=False)]
    gather x3 -> x0, local copies, waits for them, and re-layouts: 37.7 us -> none  [attend(): listed_col = jnp.take(block_flags, jnp.clip(k_pos // BLK, 0, n_blocks - 1))]
    dot_general x15 -> x0, matrix products: 35.9 us -> none  [the longest x3 11 us: attend(): jnp.einsum('tgd,kd->gtk', q_rows, window[0], preferred_element_type=jnp.f...]
    pallas_call x0 -> x3, Pallas kernels: none -> 20.8 us  [the longest x1 10.5 us: body(): pl.pallas_call(far_kernel, in_specs=[pl.BlockSpec(memory_space=pltpu.SMEM...]
    all_to_all x0 -> x3, starting transfers between devices: none -> 20.3 us  [the longest x2 15.3 us: spread(): lax.all_to_all(jnp.broadcast_to(x[None], (n,) + x.shape), axis, 0, 0, til...]
  transfers between devices with their start and end apart: 8 -> 13, of which waited for: 2 -> 4; matrix products, arithmetic and copies ran while one was open for 19% -> 4% of each run, Pallas kernels for 0% -> 5%
where the time goes in v1:
time: 216 us; the launch traced here: 215 us
  blocking collectives  61.5 us (28%)
  starting transfers between devices  54.8 us (25%)
  waiting for transfers between devices  53.9 us (25%)
  Pallas kernels  20.8 us (10%)
  between operations  13.6 us (6%)
  other arithmetic  7.16 us (3%)
  local copies, waits for them, and re-layouts  3.24 us (2%)
    all_to_all x1, blocking collectives, body(): lax.all_to_all(partial_sum.reshape(8, rows // 8, d_model), KV, 0, 0, tile...  42 us
    all_gather x1, waiting for transfers between devices, body(): w_mine = lax.all_gather(w, 'y', axis=0, tiled=False)  39.1 us
    ppermute x6, starting transfers between devices, swap(): return lax.ppermute(x, 'c', [(0, 1), (1, 0)])  23.7 us
    all_to_all x1, blocking collectives, spread(): lax.all_to_all(jnp.broadcast_to(x[None], (n,) + x.shape), axis, 0, 0, til...  19.5 us
    all_to_all x2, starting transfers between devices, spread(): lax.all_to_all(jnp.broadcast_to(x[None], (n,) + x.shape), axis, 0, 0, til...  15.3 us
    ppermute x3, starting transfers between devices, body(): own.append(lax.ppermute(own[-1], CTX, ahead))  10.7 us
    pallas_call x1, Pallas kernels, body(): pl.pallas_call(far_kernel, in_specs=[pl.BlockSpec(memory_space=pltpu.SMEM...  10.5 us
    all_to_all x2, waiting for transfers between devices, spread(): lax.all_to_all(jnp.broadcast_to(x[None], (n,) + x.shape), axis, 0, 0, til...  8.68 us
  transfers between devices with their start and end apart: 13, of which 4 were waited for; matrix products, arithmetic and copies ran while one was open for 4% of the time, Pallas kernels for 5%

profile of v1, /device:TPU:1, one launch (start us, length us, event | category | flops | bytes accessed | tf_op | source)
XLA Modules:
  0.0 215.0 jit_solution(17838845141499947944)
XLA Ops:
  7.5 19.5 %all_to_all.25 = bf16[4,64,512]{2,1,0:T(8,128)(2,1)} all-to-all(bf16[4,64,512]{2,1,0:T(8,128)(2,1)S(1)} %broadcast_in_dim.46), channel_id=1, replica_groups=mesh['zh'=4,'y'=8,'c'=2,'x'=4,'zl'=2] {'zh'}, dimensions={0} | all-to-all | bytes 524288 | tf_op jit(solution)/shard_map/all_to_all | solution.py:169
  27.8 39.1 %all-gather.3.cloned.1.call-done = bf16[32,64,512]{2,1,0:T(8,128)(2,1)} async-done(((bf16[4,64,512]{2,1,0:T(8,128)(2,1)}), bf16[32,64,512]{2,1,0:T(8,128)(2,1)}) %all-gather.3.cloned.1.call-update) | async-done | bytes 2097168 | tf_op jit(solution)/shard_map/all_gather | solution.py:216
  66.8 6.2 %collective-permute-start.8 = (bf16[8,4,64,512]{3,2,1,0:T(8,128)(2,1)}, bf16[8,4,64,512]{3,2,1,0:T(8,128)(2,1)}, u32[]{:S(2)}, u32[]{:S(2)}) collective-permute-start(bf16[8,4,64,512]{3,2,1,0:T(8,128)(2,1)} %bitcast.12), channel_id=1, source_target_pairs={{0,8},{8,0},{1,9},{9,1},{2,10},{10,2},{3,11},{11,3},{4,12},{12,4},... | collective-permute-start | bytes 6291464 | tf_op jit(solution)/shard_map/ppermute | solution.py:164
  73.1 1.3 broadcast_subtract_fusion
  74.4 1.9 pick.1
  76.2 3.1 %collective-permute-start.2 = (bf16[2,384,128]{2,1,0:T(8,128)(2,1)}, bf16[2,384,128]{2,1,0:T(8,128)(2,1)S(1)}, u32[]{:S(2)}, u32[]{:S(2)}) collective-permute-start(bf16[2,384,128]{2,1,0:T(8,128)(2,1)} %get-tuple-element.13.refs_6_), channel_id=1, source_target_pairs={{0,16},{8,24},{16,32},{24,40},{32,48},{40,56},{48,64},{56,72},{64,... | collective-permute-start | bytes 589832 | tf_op jit(solution)/shard_map/ppermute | solution.py:211
  79.3 2.2 %collective-permute-start = (bf16[8,2,64,128]{3,2,1,0:T(8,128)(2,1)}, bf16[8,2,64,128]{3,2,1,0:T(8,128)(2,1)S(1)}, u32[]{:S(2)}, u32[]{:S(2)}) collective-permute-start(bf16[8,2,64,128]{3,2,1,0:T(8,128)(2,1)} %get-tuple-element.12), channel_id=1, source_target_pairs={{0,8},{8,0},{1,9},{9,1},{2,10},{10,2},{3,11},{11,3},{4,12},{12,4},... | collective-permute-start | bytes 786440 | tf_op jit(solution)/shard_map/ppermute | solution.py:164
  83.0 1.7 add.64
  84.7 5.1 %all-to-all-start = ((bf16[8,2,64,128]{3,2,1,0:T(8,128)(2,1)}), bf16[8,2,64,128]{3,2,1,0:T(8,128)(2,1)S(1)}, u32[]{:S(2)}, u32[]{:S(2)}) async-start(bf16[8,2,64,128]{3,2,1,0:T(8,128)(2,1)} %add.64), calls=%async_computation | async-start | bytes 524288 | tf_op jit(solution)/shard_map/all_to_all | solution.py:203
  90.5 1.0 compare_reduce_fusion
  91.5 3.4 %collective-permute-start.3 = (bf16[2,384,128]{2,1,0:T(8,128)(2,1)S(1)}, bf16[2,384,128]{2,1,0:T(8,128)(2,1)S(1)}, u32[]{:S(2)}, u32[]{:S(2)}) collective-permute-start(bf16[2,384,128]{2,1,0:T(8,128)(2,1)S(1)} %collective-permute-done.2.refs_4_), channel_id=1, source_target_pairs={{0,16},{8,24},{16,32},{24,40},{32,48},{40,56},{48,64},{56,72},{64,... | collective-permute-start | bytes 589832 | tf_op jit(solution)/shard_map/ppermute | solution.py:211
  94.9 5.5 %collective-permute-done.3.refs_2_ = bf16[2,384,128]{2,1,0:T(8,128)(2,1)S(1)} collective-permute-done((bf16[2,384,128]{2,1,0:T(8,128)(2,1)S(1)}, bf16[2,384,128]{2,1,0:T(8,128)(2,1)S(1)}, u32[]{:S(2)}, u32[]{:S(2)}) %collective-permute-start.3) | collective-permute-done | bytes 196640 | tf_op jit(solution)/shard_map/ppermute | solution.py:211
  100.3 4.2 %collective-permute-start.4 = (bf16[2,384,128]{2,1,0:T(8,128)(2,1)S(1)}, bf16[2,384,128]{2,1,0:T(8,128)(2,1)S(1)}, u32[]{:S(2)}, u32[]{:S(2)}) collective-permute-start(bf16[2,384,128]{2,1,0:T(8,128)(2,1)S(1)} %collective-permute-done.3.refs_2_), channel_id=1, source_target_pairs={{0,16},{8,24},{16,32},{24,40},{32,48},{40,56},{48,64},{56,72},{64,... | collective-permute-start | bytes 589832 | tf_op jit(solution)/shard_map/ppermute | solution.py:211
  105.3 11.8 %all-to-all-start.1 = ((bf16[4,2,64,128]{3,2,1,0:T(8,128)(2,1)}), bf16[4,2,64,128]{3,2,1,0:T(8,128)(2,1)S(1)}, u32[]{:S(2)}, u32[]{:S(2)}) async-start(bf16[4,2,64,128]{3,2,1,0:T(8,128)(2,1)} %broadcast_in_dim.22), calls=%async_computation.1 | async-start | bytes 262144 | tf_op jit(solution)/shard_map/all_to_all | solution.py:169
  117.2 8.7 %all-to-all-done.1 = bf16[4,2,64,128]{3,2,1,0:T(8,128)(2,1)S(1)} async-done(((bf16[4,2,64,128]{3,2,1,0:T(8,128)(2,1)}), bf16[4,2,64,128]{3,2,1,0:T(8,128)(2,1)S(1)}, u32[]{:S(2)}, u32[]{:S(2)}) %all-to-all-start.1) | async-done | bytes 131104 | tf_op jit(solution)/shard_map/all_to_all | solution.py:169
  126.6 3.4 %all-to-all-start.2 = ((bf16[8,2,64,128]{3,2,1,0:T(8,128)(2,1)}), bf16[8,2,64,128]{3,2,1,0:T(8,128)(2,1)S(1)}, u32[]{:S(2)}, u32[]{:S(2)}) async-start(bf16[8,2,64,128]{3,2,1,0:T(8,128)(2,1)} %broadcast_in_dim.23), calls=%async_computation.2 | async-start | bytes 524288 | tf_op jit(solution)/shard_map/all_to_all | solution.py:169
  130.1 5.1 %collective-permute-start.7 = (bf16[2,384,128]{2,1,0:T(8,128)(2,1)S(1)}, bf16[2,384,128]{2,1,0:T(8,128)(2,1)S(1)}, u32[]{:S(2)}, u32[]{:S(2)}) collective-permute-start(bf16[2,384,128]{2,1,0:T(8,128)(2,1)S(1)} %get-tuple-element.19), channel_id=1, source_target_pairs={{0,8},{8,0},{1,9},{9,1},{2,10},{10,2},{3,11},{11,3},{4,12},{12,4},... | collective-permute-start | bytes 589832 | tf_op jit(solution)/shard_map/ppermute | solution.py:164
  135.3 1.9 collective-permute-start.6
  137.2 2.4 %collective-permute-start.5 = (bf16[2,384,128]{2,1,0:T(8,128)(2,1)S(1)}, bf16[2,384,128]{2,1,0:T(8,128)(2,1)S(1)}, u32[]{:S(2)}, u32[]{:S(2)}) collective-permute-start(bf16[2,384,128]{2,1,0:T(8,128)(2,1)S(1)} %get-tuple-element.21), channel_id=1, source_target_pairs={{0,8},{8,0},{1,9},{9,1},{2,10},{10,2},{3,11},{11,3},{4,12},{12,4},... | collective-permute-start | bytes 589832 | tf_op jit(solution)/shard_map/ppermute | solution.py:164
  139.8 5.9 %collective-permute-start.1 = (bf16[8,2,64,128]{3,2,1,0:T(8,128)(2,1)S(1)}, bf16[8,2,64,128]{3,2,1,0:T(8,128)(2,1)S(1)}, u32[]{:S(2)}, u32[]{:S(2)}) collective-permute-start(bf16[8,2,64,128]{3,2,1,0:T(8,128)(2,1)S(1)} %all-to-all-done.2.mine_ref), channel_id=1, source_target_pairs={{0,8},{8,0},{1,9},{9,1},{2,10},{10,2},{3,11},{11,3},{4,12},{12,4},... | collective-permute-start | bytes 786440 | tf_op jit(solution)/shard_map/ppermute | solution.py:164
  145.8 8.5 %band.1 = (f32[3,512,128]{2,1,0:T(8,128)S(1)}, f32[3,512,128]{2,1,0:T(8,128)S(1)}, f32[3,512,128]{2,1,0:T(8,128)S(1)}) custom-call(bf16[384,512]{1,0:T(8,128)(2,1)S(1)} %copy-done.1, f32[1,2176]{1,0:T(1,128)S(1)} %select_n.65.line_ref, f32[1,2688]{1,0:T(1,128)S(1)} %and_select_fusion.col_ref, bf16[2,384,128]{2,1,0:T(8,128)(2,1)S(1)} %collective-permute-done.4.refs_0_, ...), custom_call_target="tpu_custom_call" | custom-call | flops 1711276032 | bytes 8000000 | tf_op jit(solution)/shard_map/band/pallas_call | solution.py:228
  154.3 10.5 %far.1 = bf16[384,4096]{1,0:T(8,128)(2,1)} custom-call(s32[2]{0:T(128)S(1)} %pad_add_fusion.place_ref, bf16[384,512]{1,0:T(8,128)(2,1)S(1)} %copy-done.1, s32[1,1024]{1,0:T(1,128)S(1)} %add.63.pos_ref, bf16[8,2,64,128]{3,2,1,0:T(8,128)(2,1)S(1)} %all-to-all-done.2.mine_ref, bf16[8,2,64,128]{3,2,1,0:T(8,128)(2,1)S(1)} %collective-permute-done.1.other_ref, ...), custom_call_target="tpu_custom_call" | custom-call | flops 2415919104 | bytes 10000000 | tf_op jit(solution)/shard_map/far/pallas_call | solution.py:251
  164.8 42.0 %all_to_all.26 = bf16[8,48,4096]{2,1,0:T(8,128)(2,1)S(1)} all-to-all(bf16[8,48,4096]{2,1,0:T(8,128)(2,1)} %bitcast.14), channel_id=1, replica_groups=mesh['zh'=4,'y'=8,'c'=2,'x'=4,'zl'=2] {'x','zl'}, dimensions={0} | all-to-all | bytes 6291456 | tf_op jit(solution)/shard_map/all_to_all | solution.py:283
  206.8 1.3 reduce_sum.38
  (37 shorter events, 5.7 us)
Async XLA Ops:
  6.5 139.2 %copy-start.1 = (bf16[384,512]{1,0:T(8,128)(2,1)S(1)}, bf16[384,512]{1,0:T(8,128)(2,1)}, u32[]{:S(2)}) copy-start(bf16[384,512]{1,0:T(8,128)(2,1)} %q_ref.3) | copy-start | bytes 1179652
  6.5 60.3 %all-gather.3.cloned.1.call-start = ((), (), s32[]{:S(2)}) async-start(), calls=%async_computation.5 | async-start | bytes 2359296 | tf_op jit(solution)/shard_map/all_gather | solution.py:216
  66.8 87.5 %collective-permute-start.8 = (bf16[8,4,64,512]{3,2,1,0:T(8,128)(2,1)}, bf16[8,4,64,512]{3,2,1,0:T(8,128)(2,1)}, u32[]{:S(2)}, u32[]{:S(2)}) collective-permute-start(bf16[8,4,64,512]{3,2,1,0:T(8,128)(2,1)} %bitcast.12), channel_id=1, source_target_pairs={{0,8},{8,0},{1,9},{9,1},{2,10},{10,2},{3,11},{11,3},{4,12},{12,4},... | collective-permute-start | bytes 6291464 | tf_op jit(solution)/shard_map/ppermute | solution.py:164
  76.2 53.8 %copy-start.2 = (bf16[2,384,128]{2,1,0:T(8,128)(2,1)S(1)}, bf16[2,384,128]{2,1,0:T(8,128)(2,1)}, u32[]{:S(2)}) copy-start(bf16[2,384,128]{2,1,0:T(8,128)(2,1)} %get-tuple-element.13.refs_6_) | copy-start | bytes 589828
  76.2 15.2 %collective-permute-start.2 = (bf16[2,384,128]{2,1,0:T(8,128)(2,1)}, bf16[2,384,128]{2,1,0:T(8,128)(2,1)S(1)}, u32[]{:S(2)}, u32[]{:S(2)}) collective-permute-start(bf16[2,384,128]{2,1,0:T(8,128)(2,1)} %get-tuple-element.13.refs_6_), channel_id=1, source_target_pairs={{0,16},{8,24},{16,32},{24,40},{32,48},{40,56},{48,64},{56,72},{64,... | collective-permute-start | bytes 589832 | tf_op jit(solution)/shard_map/ppermute | solution.py:211
  79.3 3.6 %collective-permute-start = (bf16[8,2,64,128]{3,2,1,0:T(8,128)(2,1)}, bf16[8,2,64,128]{3,2,1,0:T(8,128)(2,1)S(1)}, u32[]{:S(2)}, u32[]{:S(2)}) collective-permute-start(bf16[8,2,64,128]{3,2,1,0:T(8,128)(2,1)} %get-tuple-element.12), channel_id=1, source_target_pairs={{0,8},{8,0},{1,9},{9,1},{2,10},{10,2},{3,11},{11,3},{4,12},{12,4},... | collective-permute-start | bytes 786440 | tf_op jit(solution)/shard_map/ppermute | solution.py:164
  84.7 19.9 %all-to-all-start = ((bf16[8,2,64,128]{3,2,1,0:T(8,128)(2,1)}), bf16[8,2,64,128]{3,2,1,0:T(8,128)(2,1)S(1)}, u32[]{:S(2)}, u32[]{:S(2)}) async-start(bf16[8,2,64,128]{3,2,1,0:T(8,128)(2,1)} %add.64), calls=%async_computation | async-start | bytes 524288 | tf_op jit(solution)/shard_map/all_to_all | solution.py:203
  91.5 8.9 %collective-permute-start.3 = (bf16[2,384,128]{2,1,0:T(8,128)(2,1)S(1)}, bf16[2,384,128]{2,1,0:T(8,128)(2,1)S(1)}, u32[]{:S(2)}, u32[]{:S(2)}) collective-permute-start(bf16[2,384,128]{2,1,0:T(8,128)(2,1)S(1)} %collective-permute-done.2.refs_4_), channel_id=1, source_target_pairs={{0,16},{8,24},{16,32},{24,40},{32,48},{40,56},{48,64},{56,72},{64,... | collective-permute-start | bytes 589832 | tf_op jit(solution)/shard_map/ppermute | solution.py:211
  100.3 29.7 %collective-permute-start.4 = (bf16[2,384,128]{2,1,0:T(8,128)(2,1)S(1)}, bf16[2,384,128]{2,1,0:T(8,128)(2,1)S(1)}, u32[]{:S(2)}, u32[]{:S(2)}) collective-permute-start(bf16[2,384,128]{2,1,0:T(8,128)(2,1)S(1)} %collective-permute-done.3.refs_2_), channel_id=1, source_target_pairs={{0,16},{8,24},{16,32},{24,40},{32,48},{40,56},{48,64},{56,72},{64,... | collective-permute-start | bytes 589832 | tf_op jit(solution)/shard_map/ppermute | solution.py:211
  105.3 20.5 %all-to-all-start.1 = ((bf16[4,2,64,128]{3,2,1,0:T(8,128)(2,1)}), bf16[4,2,64,128]{3,2,1,0:T(8,128)(2,1)S(1)}, u32[]{:S(2)}, u32[]{:S(2)}) async-start(bf16[4,2,64,128]{3,2,1,0:T(8,128)(2,1)} %broadcast_in_dim.22), calls=%async_computation.1 | async-start | bytes 262144 | tf_op jit(solution)/shard_map/all_to_all | solution.py:169
  126.6 13.2 %all-to-all-start.2 = ((bf16[8,2,64,128]{3,2,1,0:T(8,128)(2,1)}), bf16[8,2,64,128]{3,2,1,0:T(8,128)(2,1)S(1)}, u32[]{:S(2)}, u32[]{:S(2)}) async-start(bf16[8,2,64,128]{3,2,1,0:T(8,128)(2,1)} %broadcast_in_dim.23), calls=%async_computation.2 | async-start | bytes 524288 | tf_op jit(solution)/shard_map/all_to_all | solution.py:169
  130.1 15.6 %collective-permute-start.7 = (bf16[2,384,128]{2,1,0:T(8,128)(2,1)S(1)}, bf16[2,384,128]{2,1,0:T(8,128)(2,1)S(1)}, u32[]{:S(2)}, u32[]{:S(2)}) collective-permute-start(bf16[2,384,128]{2,1,0:T(8,128)(2,1)S(1)} %get-tuple-element.19), channel_id=1, source_target_pairs={{0,8},{8,0},{1,9},{9,1},{2,10},{10,2},{3,11},{11,3},{4,12},{12,4},... | collective-permute-start | bytes 589832 | tf_op jit(solution)/shard_map/ppermute | solution.py:164
  135.3 10.5 %collective-permute-start.6 = (bf16[2,384,128]{2,1,0:T(8,128)(2,1)S(1)}, bf16[2,384,128]{2,1,0:T(8,128)(2,1)S(1)}, u32[]{:S(2)}, u32[]{:S(2)}) collective-permute-start(bf16[2,384,128]{2,1,0:T(8,128)(2,1)S(1)} %get-tuple-element.20), channel_id=1, source_target_pairs={{0,8},{8,0},{1,9},{9,1},{2,10},{10,2},{3,11},{11,3},{4,12},{12,4},... | collective-permute-start | bytes 589832 | tf_op jit(solution)/shard_map/ppermute | solution.py:164
  137.2 8.6 %collective-permute-start.5 = (bf16[2,384,128]{2,1,0:T(8,128)(2,1)S(1)}, bf16[2,384,128]{2,1,0:T(8,128)(2,1)S(1)}, u32[]{:S(2)}, u32[]{:S(2)}) collective-permute-start(bf16[2,384,128]{2,1,0:T(8,128)(2,1)S(1)} %get-tuple-element.21), channel_id=1, source_target_pairs={{0,8},{8,0},{1,9},{9,1},{2,10},{10,2},{3,11},{11,3},{4,12},{12,4},... | collective-permute-start | bytes 589832 | tf_op jit(solution)/shard_map/ppermute | solution.py:164
  139.8 14.5 %collective-permute-start.1 = (bf16[8,2,64,128]{3,2,1,0:T(8,128)(2,1)S(1)}, bf16[8,2,64,128]{3,2,1,0:T(8,128)(2,1)S(1)}, u32[]{:S(2)}, u32[]{:S(2)}) collective-permute-start(bf16[8,2,64,128]{3,2,1,0:T(8,128)(2,1)S(1)} %all-to-all-done.2.mine_ref), channel_id=1, source_target_pairs={{0,8},{8,0},{1,9},{9,1},{2,10},{10,2},{3,11},{11,3},{4,12},{12,4},... | collective-permute-start | bytes 786440 | tf_op jit(solution)/shard_map/ppermute | solution.py:164
  145.8 8.6 %copy-start = (bf16[32,64,512]{2,1,0:T(8,128)(2,1)S(1)}, bf16[32,64,512]{2,1,0:T(8,128)(2,1)}, u32[]{:S(2)}) copy-start(bf16[32,64,512]{2,1,0:T(8,128)(2,1)} %all-gather.3.cloned.1.call-done) | copy-start | bytes 6291460
Sparse Core Ops, SparseCore 0:
  27.1 39.7 all-gather.2

commit v2 on v1

v2 whole, which is shorter than its diff:
```python
import functools
import math

import jax
import jax.numpy as jnp
from jax import lax
from jax.experimental import pallas as pl
from jax.experimental.pallas import tpu as pltpu
from jax.sharding import Mesh, PartitionSpec as P

BLK = 64
SLASH_MAX = 2048
HD = 128
GROUP = 4
QB = 128
MASKED = -1e30
CTX = ("zh", "y", "c")
KV = ("x", "zl")
ZY = ("zh", "y")
SCALE = math.log2(math.e) / math.sqrt(HD)
NT = (((1,), (1,)), ((), ()))
VMEM_LIMIT = 48 * 1024 * 1024


def vmem(n):
    return [pl.BlockSpec(memory_space=pltpu.VMEM)] * n


def pick_kernel(place_ref, listed_ref, k_ref, v_ref, pair_ref, keep_ref, send_ref):
    rows = k_ref.shape[0]
    base = place_ref[0] * (rows // BLK)
    flip = place_ref[1] * keep_ref.shape[0]
    pair_ref[0] = k_ref[...]
    pair_ref[1] = v_ref[...]
    half = keep_ref.shape[0]
    for slot in range(2 * half):
        block = listed_ref[0, (slot + flip) % (2 * half)] - base
        here = jnp.logical_and(block >= 0, block < rows // BLK)
        row = pl.multiple_of(jnp.clip(block, 0, rows // BLK - 1) * BLK, BLK)
        out = keep_ref if slot < half else send_ref
        for part, ref in enumerate((k_ref, v_ref)):
            got = ref[pl.ds(row, BLK), :].astype(jnp.float32)
            out[slot % half, part] = jnp.where(here, got, 0.0).astype(jnp.bfloat16)


def choose_kernel(place_ref, *refs):
    own, out_ref = refs[:4], refs[4]
    for core in (0, 1):
        @pl.when(place_ref[1] == core)
        def _(core=core):
            for k in range(3):
                out_ref[k] = own[k + core][...]


def total_kernel(x_ref, *refs):
    out_ref = refs[-1]
    total = jnp.sum(x_ref[...].astype(jnp.float32), axis=0).astype(jnp.bfloat16)
    for i in range(out_ref.shape[0]):
        out_ref[i] = total


def stacked_queries(q_ref, first):
    return jnp.concatenate(
        [q_ref[pl.ds(first, QB), h * HD : (h + 1) * HD] for h in range(GROUP)], axis=0
    )


def lane_fold(op, x):
    out = x[:, :HD]
    for i in range(1, x.shape[1] // HD):
        out = op(out, x[:, i * HD : (i + 1) * HD])
    return out


def collect_kernel(place_ref, own, up, down, far_lo, far_hi, late, later, out_ref, sems):
    n_zh, n_y = out_ref.shape[:2]
    me = place_ref[0] // (2 * n_y)
    mid = n_y // 2
    far = out_ref.at[lax.rem(me + 2, n_zh)]
    pieces = (
        (own, out_ref.at[me]),
        (up, out_ref.at[lax.rem(me + n_zh - 1, n_zh)]),
        (down, out_ref.at[lax.rem(me + 1, n_zh)]),
        (far_lo, far.at[:mid]),
        (far_hi, far.at[mid:]),
    )
    copies = [pltpu.make_async_copy(a, b, sems.at[i]) for i, (a, b) in enumerate(pieces)]
    for copy in copies:
        copy.start()
    for copy in copies:
        copy.wait()


def band_kernel(place_ref, listed_ref, q_ref, slash_ref, *refs):
    own, other = refs[:4], refs[4]
    (acc_ref, top_ref, sum_ref), (diag, col, bias, kwin, vwin, s_scr) = refs[5:8], refs[8:]
    rows = q_ref.shape[0]
    span = SLASH_MAX + QB
    lead = 7 * rows - rows - SLASH_MAX
    for i in range(7):
        piece = own[3 - i // 2] if i % 2 == 0 else other.at[2 - i // 2]
        kwin[i * rows : (i + 1) * rows] = piece[0]
        vwin[i * rows : (i + 1) * rows] = piece[1]

    at = SLASH_MAX - slash_ref[...]
    n_off = at.shape[1]
    major = lax.broadcasted_iota(jnp.int32, (32, n_off), 0) == at // HD
    minor = lax.broadcasted_iota(jnp.int32, (HD, n_off), 0) == at % HD
    hits = lax.dot_general(
        jnp.where(major, 1.0, 0.0).astype(jnp.bfloat16),
        jnp.where(minor, 1.0, 0.0).astype(jnp.bfloat16),
        NT,
        preferred_element_type=jnp.float32,
    )
    line = jnp.where(hits > 0.5, 0.0, MASKED)
    for i in range(span // HD):
        bias[:, i * HD : (i + 1) * HD] = jnp.broadcast_to(line[i : i + 1], (QB, HD))
    diag[...] = pltpu.roll(bias[...], 0, 1, stride=1, stride_axis=0)

    block = lax.broadcasted_iota(jnp.int32, (1, 7 * rows), 1) // BLK
    block = block + (place_ref[0] - 6) * (rows // BLK)
    out = block < 0
    for i in range(listed_ref.shape[1]):
        out = jnp.logical_or(out, block == listed_ref[0, i])
    col[...] = jnp.where(out, MASKED, 0.0)

    chunks = [(at, min(256, span - at)) for at in range(0, span, 256)]

    @pl.loop(0, rows // QB)
    def _(step):
        first = pl.multiple_of(step * QB, QB)
        base = pl.multiple_of(lead + step * QB, QB)
        bias[...] = diag[...] + col[:, pl.ds(base, span)]
        q = stacked_queries(q_ref, first)
        top = jnp.full((GROUP * QB, HD), MASKED, jnp.float32)
        for at, width in chunks:
            k = kwin[pl.ds(base + at, width), :]
            s = lax.dot_general(q, k, NT, preferred_element_type=jnp.float32)
            b = bias[:, at : at + width]
            s = s + jnp.concatenate([b] * GROUP, axis=0)
            s_scr[:, at : at + width] = s
            top = jnp.maximum(top, lane_fold(jnp.maximum, s))
        top = jnp.max(top, axis=1, keepdims=True)
        shift = top * SCALE
        acc = jnp.zeros((GROUP * QB, HD), jnp.float32)
        total = jnp.zeros((GROUP * QB, HD), jnp.float32)
        for at, width in chunks:
            p = jnp.exp2(s_scr[:, at : at + width] * SCALE - shift)
            total = total + lane_fold(jnp.add, p)
            v = vwin[pl.ds(base + at, width), :]
            acc = acc + jnp.dot(p.astype(jnp.bfloat16), v, preferred_element_type=jnp.float32)
        acc_ref[step] = acc
        sum_ref[step] = total
        top_ref[step] = jnp.broadcast_to(top, (GROUP * QB, HD))


def far_kernel(place_ref, listed_ref, q_ref, mine_ref, other_ref, acc_ref, top_ref, sum_ref,
               attended, kfar, vfar):
    rows = q_ref.shape[0]
    half = mine_ref.shape[0]
    flip = place_ref[1] * half
    for i in range(half):
        for j, ref in enumerate((mine_ref, other_ref)):
            at = (j * half + i) * BLK
            kfar[at : at + BLK] = ref[i, 0]
            vfar[at : at + BLK] = ref[i, 1]
    n_far = kfar.shape[0]
    chunks = [(at, 256) for at in range(0, n_far, 256)]
    lane = lax.broadcasted_iota(jnp.int32, (1, 256), 1)
    positions = []
    for at, width in chunks:
        pos = jnp.zeros((1, 256), jnp.int32)
        for i in range(width // BLK):
            slot = (at // BLK + i + flip) % (2 * half)
            pos = jnp.where(lane // BLK == i, listed_ref[0, slot], pos)
        positions.append(pos * BLK + lane % BLK)

    @pl.loop(0, rows // QB)
    def _(step):
        first = pl.multiple_of(step * QB, QB)
        q = stacked_queries(q_ref, first)
        q_pos = place_ref[0] * rows + first + lax.broadcasted_iota(jnp.int32, (QB, 256), 0)
        band_top = top_ref[step]
        top = band_top
        scores = []
        for (at, width), pos in zip(chunks, positions):
            s = lax.dot_general(q, kfar[at : at + width], NT, preferred_element_type=jnp.float32)
            b = jnp.where(pos <= q_pos, 0.0, MASKED)
            s = s + jnp.concatenate([b] * GROUP, axis=0)
            scores.append(s)
            top = jnp.maximum(top, lane_fold(jnp.maximum, s))
        top = jnp.max(top, axis=1, keepdims=True)
        shift = top * SCALE
        fade = jnp.exp2(band_top * SCALE - shift)
        acc = acc_ref[step] * fade
        total = sum_ref[step] * fade
        for (at, width), s in zip(chunks, scores):
            p = jnp.exp2(s * SCALE - shift)
            total = total + lane_fold(jnp.add, p)
            acc = acc + jnp.dot(
                p.astype(jnp.bfloat16), vfar[at : at + width], preferred_element_type=jnp.float32
            )
        out = (acc / jnp.sum(total, axis=1, keepdims=True)).astype(jnp.bfloat16)
        for h in range(GROUP):
            attended[pl.ds(first, QB), h * HD : (h + 1) * HD] = out[h * QB : (h + 1) * QB]


def project_kernel(place_ref, att_ref, w_mine, w_other, out_ref, w_scr, sem_in, out_scr, sem_out):
    core = place_ref[1]
    n_zh, n_y = w_mine.shape[0], w_mine.shape[1]
    width = 512
    per = width // w_scr.shape[2] // 2
    span = out_ref.shape[1] // n_zh

    def fetch(z, i):
        src, at = ((w_mine, core), (w_other, 1 - core))[i]
        dst = w_scr.at[pl.ds(z * n_y, n_y), at]
        return pltpu.make_async_copy(src.at[z], dst, sem_in.at[z, i])

    def store(z):
        return pltpu.make_async_copy(
            out_scr.at[z], out_ref.at[:, z * span : (z + 1) * span], sem_out.at[z]
        )

    for z in range(n_zh):
        fetch(z, 0).start()
        fetch(z, 1).start()
    for z in range(n_zh):
        fetch(z, 0).wait()
        fetch(z, 1).wait()
        for n in range(span // width):
            w = w_scr[z * n_y + n * per : z * n_y + (n + 1) * per].reshape(width, GROUP * HD)
            out_scr[z, :, n * width : (n + 1) * width] = lax.dot_general(
                att_ref[...], w, NT, preferred_element_type=jnp.float32
            ).astype(jnp.bfloat16)
        store(z).start()
    for z in range(n_zh):
        store(z).wait()


def after(x, *others):
    return pl.pallas_call(
        lambda *refs: None,
        in_specs=[pl.BlockSpec(memory_space=pl.ANY)] * (1 + len(others)),
        out_specs=pl.BlockSpec(memory_space=pl.ANY),
        out_shape=jax.ShapeDtypeStruct(x.shape, x.dtype),
        input_output_aliases={0: 0},
        name="after",
    )(x, *others)


def swap(x):
    return lax.ppermute(x, "c", [(0, 1), (1, 0)])


def spread(x, axis):
    n = lax.axis_size(axis)
    return lax.all_to_all(jnp.broadcast_to(x[None], (n,) + x.shape), axis, 0, 0, tiled=True)


def summed(x):
    return jnp.sum(x.astype(jnp.float32), axis=0).astype(jnp.bfloat16)


def body(query, keys, values, vertical, slash, out_weight):
    rows, width = keys.shape
    n_ctx = lax.axis_size(CTX)
    n_y, n_zh = lax.axis_size("y"), lax.axis_size("zh")
    place = lax.axis_index(CTX)
    core = lax.axis_index("c")
    half = vertical.shape[1] // 2
    cols, inner = out_weight.shape[1], out_weight.shape[0]
    span = SLASH_MAX + QB
    bf16, f32 = jnp.bfloat16, jnp.float32
    smem = [pl.BlockSpec(memory_space=pltpu.SMEM)]
    hbm = [pl.BlockSpec(memory_space=pl.ANY)]
    where = jnp.stack([place, core]).astype(jnp.int32)

    def shape(*dims, dtype=bf16):
        return jax.ShapeDtypeStruct(dims, dtype)

    pair, keep, send = pl.pallas_call(
        pick_kernel,
        in_specs=smem * 2 + vmem(2),
        out_specs=vmem(3),
        out_shape=[
            shape(2, rows, width),
            shape(half, 2, BLK, width),
            shape(half, 2, BLK, width),
        ],
        name="pick",
    )(where, vertical, keys, values)

    up = [(i, (i + 1) % n_zh) for i in range(n_zh)]
    down = [(i, (i - 1) % n_zh) for i in range(n_zh)]
    w = spread(out_weight.T, "y")
    w_up = lax.ppermute(w, "zh", up)
    w_down = lax.ppermute(w, "zh", down)

    own = [pair]
    for k in (1, 2, 3):
        own.append(lax.ppermute(pair, CTX, [(i, i + 2 * k) for i in range(n_ctx - 2 * k)]))

    blocks = (keep + swap(send)).reshape(n_zh * n_y, -1, width)
    parts = lax.all_to_all(after(blocks, w), ZY, 0, 0, tiled=True)
    parts = pl.pallas_call(
        total_kernel, in_specs=vmem(1) + hbm * 5, out_specs=vmem(1)[0],
        out_shape=shape(*parts.shape), name="total",
    )(parts, w_up, w_down, *own[1:])
    far_mine = lax.all_to_all(parts, ZY, 0, 0, tiled=True).reshape(half, 2, BLK, width)
    far_other = swap(far_mine)

    other = swap(pl.pallas_call(
        choose_kernel, in_specs=smem + vmem(4), out_specs=vmem(1)[0],
        out_shape=shape(3, 2, rows, width), name="choose",
    )(where, *own))

    steps = rows // QB
    stats = shape(steps, GROUP * QB, HD, dtype=f32)
    acc, top, total = pl.pallas_call(
        band_kernel,
        in_specs=smem * 2 + vmem(7),
        out_specs=vmem(3),
        out_shape=[stats, stats, stats],
        scratch_shapes=[
            pltpu.VMEM((QB, span), f32),
            pltpu.VMEM((1, 7 * rows), f32),
            pltpu.VMEM((QB, span), f32),
            pltpu.VMEM((7 * rows, HD), bf16),
            pltpu.VMEM((7 * rows, HD), bf16),
            pltpu.VMEM((GROUP * QB, span), f32),
        ],
        compiler_params=pltpu.CompilerParams(vmem_limit_bytes=VMEM_LIMIT),
        cost_estimate=pl.CostEstimate(
            flops=8 * rows * GROUP * HD * span,
            bytes_accessed=8_000_000,
            transcendentals=rows * GROUP * span,
        ),
        name="band",
    )(where, vertical, query, slash, *own, other)

    mid = n_y // 2
    w_mine = pl.pallas_call(
        collect_kernel,
        in_specs=smem + hbm * 7,
        out_specs=hbm[0],
        out_shape=shape(n_zh, *w.shape),
        scratch_shapes=[pltpu.SemaphoreType.DMA((5,))],
        name="collect",
    )(
        where, w, w_up, w_down,
        lax.ppermute(w_up[:mid], "zh", up),
        lax.ppermute(w_down[mid:], "zh", down),
        far_mine, acc,
    )
    w_other = swap(w_mine)

    n_far = 2 * half * BLK
    attended = pl.pallas_call(
        far_kernel,
        in_specs=smem * 2 + vmem(6),
        out_specs=vmem(1)[0],
        out_shape=shape(rows, GROUP * HD),
        scratch_shapes=[pltpu.VMEM((n_far, HD), bf16), pltpu.VMEM((n_far, HD), bf16)],
        compiler_params=pltpu.CompilerParams(vmem_limit_bytes=VMEM_LIMIT),
        cost_estimate=pl.CostEstimate(
            flops=8 * rows * GROUP * HD * n_far,
            bytes_accessed=8_000_000,
            transcendentals=rows * GROUP * n_far,
        ),
        name="far",
    )(where, vertical, query, far_mine, far_other, acc, top, total)

    d_model = cols * n_ctx
    partial_sum = pl.pallas_call(
        project_kernel,
        in_specs=smem + vmem(1) + hbm * 2,
        out_specs=hbm[0],
        out_shape=shape(rows, d_model),
        scratch_shapes=[
            pltpu.VMEM((n_zh * n_y, 2, cols, inner), bf16),
            pltpu.SemaphoreType.DMA((n_zh, 2)),
            pltpu.VMEM((n_zh, rows, d_model // n_zh), bf16),
            pltpu.SemaphoreType.DMA((n_zh,)),
        ],
        compiler_params=pltpu.CompilerParams(vmem_limit_bytes=VMEM_LIMIT),
        cost_estimate=pl.CostEstimate(
            flops=2 * rows * inner * d_model, bytes_accessed=8_000_000, transcendentals=0
        ),
        name="project",
    )(where, attended, w_mine, w_other)
    received = lax.all_to_all(partial_sum.reshape(8, rows // 8, d_model), KV, 0, 0, tiled=True)
    return summed(received)


def solution(mesh):
    fine = Mesh(mesh.devices.reshape(4, 8, 2, 4, 2), CTX + KV)
    return jax.shard_map(
        body,
        mesh=fine,
        in_specs=(
            P(CTX, KV),
            P(CTX, KV),
            P(CTX, KV),
            P(KV, None),
            P(KV, None),
            P(KV, CTX),
        ),
        out_specs=P(CTX + KV, None),
        check_vma=False,
    )
```

time: 216 us -> 253 us (1.17)
  Pallas kernels: 20.8 us -> 90.3 us
  blocking collectives: 61.5 us -> 41.3 us
  waiting for transfers between devices: 53.9 us -> 36.3 us
  starting transfers between devices: 54.8 us -> 68.5 us
  between operations: 13.6 us -> 0.36 us
  local copies, waits for them, and re-layouts: 3.24 us -> 10.6 us
  other arithmetic: 7.16 us -> 3.65 us
    pallas_call x3 -> x8, Pallas kernels: 20.8 us -> 90.3 us  [the longest x1 65.3 us: body(): pl.pallas_call(collect_kernel, in_specs=smem + hbm * 7, out_specs=hbm[0],...]
    all_gather x1 -> x0, waiting for transfers between devices: 39.1 us -> none  [body(): w_mine = lax.all_gather(w, 'y', axis=0, tiled=False)]
    all_to_all x1 -> x2, waiting for transfers between devices: 0.01 us -> 30.4 us  [the longest x1 30.4 us: body(): parts = lax.all_to_all(after(blocks, w), ZY, 0, 0, tiled=True)]
    ppermute x3 -> x7, starting transfers between devices: 10.7 us -> 30.7 us  [the longest x3 11.9 us: body(): lax.ppermute(pair, CTX, [(i, i + 2 * k) for i in range(n_ctx - 2 * k)])]
    all_to_all x1 -> x0, blocking collectives: 19.5 us -> none  [spread(): lax.all_to_all(jnp.broadcast_to(x[None], (n,) + x.shape), axis, 0, 0, til...]
    all_to_all x2 -> x1, waiting for transfers between devices: 8.68 us -> 0.01 us  [spread(): lax.all_to_all(jnp.broadcast_to(x[None], (n,) + x.shape), axis, 0, 0, til...]
    all_to_all x2 -> x1, starting transfers between devices: 15.3 us -> 7.65 us  [spread(): lax.all_to_all(jnp.broadcast_to(x[None], (n,) + x.shape), axis, 0, 0, til...]
    all_to_all x1 -> x2, starting transfers between devices: 5.07 us -> 12.1 us  [the longest x1 8.25 us: body(): parts = lax.all_to_all(after(blocks, w), ZY, 0, 0, tiled=True)]
  transfers between devices with their start and end apart: 13 -> 14, of which waited for: 4 -> 4; matrix products, arithmetic and copies ran while one was open for 4% -> 2% of each run, Pallas kernels for 5% -> 8%
where the time goes in v2:
time: 253 us; the launch traced here: 251 us
  Pallas kernels  90.3 us (36%)
  starting transfers between devices  68.5 us (27%)
  blocking collectives  41.3 us (16%)
  waiting for transfers between devices  36.3 us (14%)
  local copies, waits for them, and re-layouts  10.6 us (4%)
  other arithmetic  3.65 us (1%)
    pallas_call x1, Pallas kernels, body(): pl.pallas_call(collect_kernel, in_specs=smem + hbm * 7, out_specs=hbm[0],...  65.3 us
    all_to_all x1, blocking collectives, body(): lax.all_to_all(partial_sum.reshape(8, rows // 8, d_model), KV, 0, 0, tile...  41.3 us
    all_to_all x1, waiting for transfers between devices, body(): parts = lax.all_to_all(after(blocks, w), ZY, 0, 0, tiled=True)  30.4 us
    ppermute x4, starting transfers between devices, swap(): return lax.ppermute(x, 'c', [(0, 1), (1, 0)])  18.1 us
    ppermute x3, starting transfers between devices, body(): lax.ppermute(pair, CTX, [(i, i + 2 * k) for i in range(n_ctx - 2 * k)])  11.9 us
    ppermute x1, starting transfers between devices, body(): w_down = lax.ppermute(w, 'zh', down)  9.67 us
    pallas_call x1, Pallas kernels, body(): pl.pallas_call(band_kernel, in_specs=smem * 2 + vmem(7), out_specs=vmem(3...  9.57 us
    all_to_all x1, starting transfers between devices, body(): parts = lax.all_to_all(after(blocks, w), ZY, 0, 0, tiled=True)  8.25 us
  transfers between devices with their start and end apart: 14, of which 4 were waited for; matrix products, arithmetic and copies ran while one was open for 2% of the time, Pallas kernels for 8%

profile of v2, /device:TPU:1, one launch (start us, length us, event | category | flops | bytes accessed | tf_op | source)
XLA Modules:
  0.0 251.2 jit_solution(7992885513741718050)
XLA Ops:
  1.7 7.7 %all-to-all-start = ((bf16[8,64,512]{2,1,0:T(8,128)(2,1)}), bf16[8,64,512]{2,1,0:T(8,128)(2,1)S(1)}, u32[]{:S(2)}, u32[]{:S(2)}) async-start(bf16[8,64,512]{2,1,0:T(8,128)(2,1)} %broadcast_in_dim.2), calls=%async_computation | async-start | bytes 1048576 | tf_op jit(solution)/shard_map/all_to_all | solution.py:258
  9.9 1.9 pick.1
  11.9 4.6 %collective-permute-start = (bf16[8,2,64,128]{3,2,1,0:T(8,128)(2,1)}, bf16[8,2,64,128]{3,2,1,0:T(8,128)(2,1)S(1)}, u32[]{:S(2)}, u32[]{:S(2)}) collective-permute-start(bf16[8,2,64,128]{3,2,1,0:T(8,128)(2,1)} %get-tuple-element.12), channel_id=1, source_target_pairs={{0,8},{8,0},{1,9},{9,1},{2,10},{10,2},{3,11},{11,3},{4,12},{12,4},... | collective-permute-start | bytes 786440 | tf_op jit(solution)/shard_map/ppermute | solution.py:253
  16.5 5.4 %collective-permute-start.5 = (bf16[2,384,128]{2,1,0:T(8,128)(2,1)}, bf16[2,384,128]{2,1,0:T(8,128)(2,1)S(1)}, u32[]{:S(2)}, u32[]{:S(2)}) collective-permute-start(bf16[2,384,128]{2,1,0:T(8,128)(2,1)} %get-tuple-element.13.refs_0_), channel_id=1, source_target_pairs={{0,48},{8,56},{16,64},{24,72},{32,80},{40,88},{48,96},{56,104},{64... | collective-permute-start | bytes 589832 | tf_op jit(solution)/shard_map/ppermute | solution.py:302
  21.9 4.3 %collective-permute-start.4 = (bf16[2,384,128]{2,1,0:T(8,128)(2,1)}, bf16[2,384,128]{2,1,0:T(8,128)(2,1)S(1)}, u32[]{:S(2)}, u32[]{:S(2)}) collective-permute-start(bf16[2,384,128]{2,1,0:T(8,128)(2,1)} %get-tuple-element.13.refs_0_), channel_id=1, source_target_pairs={{0,32},{8,40},{16,48},{24,56},{32,64},{40,72},{48,80},{56,88},{64,... | collective-permute-start | bytes 589832 | tf_op jit(solution)/shard_map/ppermute | solution.py:302
  26.2 2.2 collective-permute-start.3
  28.4 9.7 %collective-permute-start.2 = (bf16[8,64,512]{2,1,0:T(8,128)(2,1)S(1)}, bf16[8,64,512]{2,1,0:T(8,128)(2,1)S(1)}, u32[]{:S(2)}, u32[]{:S(2)}) collective-permute-start(bf16[8,64,512]{2,1,0:T(8,128)(2,1)S(1)} %all-to-all-done.refs_1_.own), channel_id=1, source_target_pairs={{0,384},{128,0},{256,128},{384,256},{1,385},{129,1},{257,129},{385... | collective-permute-start | bytes 1572872 | tf_op jit(solution)/shard_map/ppermute | solution.py:298
  38.1 1.9 collective-permute-start.1
  41.8 8.2 %all-to-all-start.1 = ((bf16[32,32,128]{2,1,0:T(8,128)(2,1)}), bf16[32,32,128]{2,1,0:T(8,128)(2,1)S(1)}, u32[]{:S(2)}, u32[]{:S(2)}) async-start(bf16[32,32,128]{2,1,0:T(8,128)(2,1)} %after.1), calls=%async_computation.1 | async-start | bytes 524288 | tf_op jit(solution)/shard_map/all_to_all | solution.py:305
  51.5 2.1 choose.1
  53.6 8.6 %collective-permute-start.7 = (bf16[3,2,384,128]{3,2,1,0:T(8,128)(2,1)}, bf16[3,2,384,128]{3,2,1,0:T(8,128)(2,1)S(1)}, u32[]{:S(2)}, u32[]{:S(2)}) collective-permute-start(bf16[3,2,384,128]{3,2,1,0:T(8,128)(2,1)} %choose.1), channel_id=1, source_target_pairs={{0,8},{8,0},{1,9},{9,1},{2,10},{10,2},{3,11},{11,3},{4,12},{12,4},... | collective-permute-start | bytes 1769480 | tf_op jit(solution)/shard_map/ppermute | solution.py:253
  62.2 30.4 %all-to-all-done.1.x_ref = bf16[32,32,128]{2,1,0:T(8,128)(2,1)S(1)} async-done(((bf16[32,32,128]{2,1,0:T(8,128)(2,1)}), bf16[32,32,128]{2,1,0:T(8,128)(2,1)S(1)}, u32[]{:S(2)}, u32[]{:S(2)}) %all-to-all-start.1) | async-done | bytes 262176 | tf_op jit(solution)/shard_map/all_to_all | solution.py:305
  95.2 3.9 %all-to-all-start.2 = ((bf16[32,32,128]{2,1,0:T(8,128)(2,1)}), bf16[32,32,128]{2,1,0:T(8,128)(2,1)S(1)}, u32[]{:S(2)}, u32[]{:S(2)}) async-start(bf16[32,32,128]{2,1,0:T(8,128)(2,1)} %total.1), calls=%async_computation.2 | async-start | bytes 524288 | tf_op jit(solution)/shard_map/all_to_all | solution.py:310
  100.1 5.3 %collective-permute-start.9 = (bf16[4,64,512]{2,1,0:T(8,128)(2,1)S(1)}, bf16[4,64,512]{2,1,0:T(8,128)(2,1)S(1)}, u32[]{:S(2)}, u32[]{:S(2)}) collective-permute-start(bf16[4,64,512]{2,1,0:T(8,128)(2,1)S(1)} %slice.9), channel_id=1, source_target_pairs={{0,384},{128,0},{256,128},{384,256},{1,385},{129,1},{257,129},{385... | collective-permute-start | bytes 786440 | tf_op jit(solution)/shard_map/ppermute | solution.py:353
  106.4 1.9 collective-permute-start.8
  108.4 9.6 %band.1 = (f32[3,512,128]{2,1,0:T(8,128)S(1)}, f32[3,512,128]{2,1,0:T(8,128)S(1)}, f32[3,512,128]{2,1,0:T(8,128)S(1)}) custom-call(s32[2]{0:T(128)S(1)} %copy-done.12, s32[1,16]{1,0:T(1,128)S(1)} %copy-done.14, bf16[384,512]{1,0:T(8,128)(2,1)S(1)} %copy-done.15, s32[1,768]{1,0:T(1,128)S(1)} %copy-done.16, bf16[2,384,128]{2,1,0:T(8,128)(2,1)S(1)} %copy-done.11, ...), custom_call_target="tpu_custom_call" | custom-call | flops 3422552064 | bytes 8000000 | tf_op jit(solution)/shard_map/band/pallas_call | solution.py:320
  120.6 2.6 %collective-permute-done.8.far_lo = bf16[4,64,512]{2,1,0:T(8,128)(2,1)S(1)} collective-permute-done((bf16[4,64,512]{2,1,0:T(8,128)(2,1)S(1)}, bf16[4,64,512]{2,1,0:T(8,128)(2,1)S(1)}, u32[]{:S(2)}, u32[]{:S(2)}) %collective-permute-start.8) | collective-permute-done | bytes 262176 | tf_op jit(solution)/shard_map/ppermute | solution.py:352
  124.1 65.3 %collect.1.w_mine = bf16[4,8,64,512]{3,2,1,0:T(8,128)(2,1)} custom-call(s32[2]{0:T(128)} %pad_add_fusion.place_ref, bf16[8,64,512]{2,1,0:T(8,128)(2,1)} %copy-done.19, bf16[8,64,512]{2,1,0:T(8,128)(2,1)} %collective-permute-done.1.refs_0_.up, bf16[8,64,512]{2,1,0:T(8,128)(2,1)} %copy-done.20, bf16[4,64,512]{2,1,0:T(8,128)(2,1)} %copy-done.23, ...), custom_call_target="tpu_custom_call" | custom-call | tf_op jit(solution)/shard_map/collect/pallas_call | solution.py:343
  189.4 3.0 %collective-permute-start.10 = (bf16[4,8,64,512]{3,2,1,0:T(8,128)(2,1)}, bf16[4,8,64,512]{3,2,1,0:T(8,128)(2,1)S(1)}, u32[]{:S(2)}, u32[]{:S(2)}) collective-permute-start(bf16[4,8,64,512]{3,2,1,0:T(8,128)(2,1)} %collect.1.w_mine), channel_id=1, source_target_pairs={{0,8},{8,0},{1,9},{9,1},{2,10},{10,2},{3,11},{11,3},{4,12},{12,4},... | collective-permute-start | bytes 6291464 | tf_op jit(solution)/shard_map/ppermute | solution.py:253
  192.4 1.9 collective-permute-start.6
  194.3 2.4 collective-permute-done.6.other_ref
  198.8 5.4 %far.1.att_ref = bf16[384,512]{1,0:T(8,128)(2,1)S(1)} custom-call(s32[2]{0:T(128)S(1)} %copy-done.13, s32[1,16]{1,0:T(1,128)S(1)} %copy-done.14, bf16[384,512]{1,0:T(8,128)(2,1)S(1)} %copy-done.15, bf16[8,2,64,128]{3,2,1,0:T(8,128)(2,1)S(1)} %bitcast.8, bf16[8,2,64,128]{3,2,1,0:T(8,128)(2,1)S(1)} %collective-permute-done.6.other_ref, ...), custom_call_target="tpu_custom_call" | custom-call | flops 1610612736 | bytes 8000000 | tf_op jit(solution)/shard_map/far/pallas_call | solution.py:359
  204.2 4.3 %project.1 = bf16[384,4096]{1,0:T(8,128)(2,1)} custom-call(s32[2]{0:T(128)S(1)} %copy-done.13, bf16[384,512]{1,0:T(8,128)(2,1)S(1)} %far.1.att_ref, bf16[4,8,64,512]{3,2,1,0:T(8,128)(2,1)S(1)} %copy-done, bf16[4,8,64,512]{3,2,1,0:T(8,128)(2,1)S(1)} %collective-permute-done.10.w_other), custom_call_target="tpu_custom_call" | custom-call | flops 1610612736 | bytes 8000000 | tf_op jit(solution)/shard_map/project/pallas_call | solution.py:375
  208.5 41.3 %all_to_all.20 = bf16[8,48,4096]{2,1,0:T(8,128)(2,1)S(1)} all-to-all(bf16[8,48,4096]{2,1,0:T(8,128)(2,1)} %bitcast.9), channel_id=1, replica_groups=mesh['zh'=4,'y'=8,'c'=2,'x'=4,'zl'=2] {'x','zl'}, dimensions={0} | all-to-all | bytes 6291456 | tf_op jit(solution)/shard_map/all_to_all | solution.py:392
  (67 shorter events, 16.9 us)
Async XLA Ops:
  1.7 26.7 %all-to-all-start = ((bf16[8,64,512]{2,1,0:T(8,128)(2,1)}), bf16[8,64,512]{2,1,0:T(8,128)(2,1)S(1)}, u32[]{:S(2)}, u32[]{:S(2)}) async-start(bf16[8,64,512]{2,1,0:T(8,128)(2,1)} %broadcast_in_dim.2), calls=%async_computation | async-start | bytes 1048576 | tf_op jit(solution)/shard_map/all_to_all | solution.py:258
  11.9 26.2 %collective-permute-start = (bf16[8,2,64,128]{3,2,1,0:T(8,128)(2,1)}, bf16[8,2,64,128]{3,2,1,0:T(8,128)(2,1)S(1)}, u32[]{:S(2)}, u32[]{:S(2)}) collective-permute-start(bf16[8,2,64,128]{3,2,1,0:T(8,128)(2,1)} %get-tuple-element.12), channel_id=1, source_target_pairs={{0,8},{8,0},{1,9},{9,1},{2,10},{10,2},{3,11},{11,3},{4,12},{12,4},... | collective-permute-start | bytes 786440 | tf_op jit(solution)/shard_map/ppermute | solution.py:253
  16.5 33.6 %collective-permute-start.5 = (bf16[2,384,128]{2,1,0:T(8,128)(2,1)}, bf16[2,384,128]{2,1,0:T(8,128)(2,1)S(1)}, u32[]{:S(2)}, u32[]{:S(2)}) collective-permute-start(bf16[2,384,128]{2,1,0:T(8,128)(2,1)} %get-tuple-element.13.refs_0_), channel_id=1, source_target_pairs={{0,48},{8,56},{16,64},{24,72},{32,80},{40,88},{48,96},{56,104},{64... | collective-permute-start | bytes 589832 | tf_op jit(solution)/shard_map/ppermute | solution.py:302
  21.9 28.2 %collective-permute-start.4 = (bf16[2,384,128]{2,1,0:T(8,128)(2,1)}, bf16[2,384,128]{2,1,0:T(8,128)(2,1)S(1)}, u32[]{:S(2)}, u32[]{:S(2)}) collective-permute-start(bf16[2,384,128]{2,1,0:T(8,128)(2,1)} %get-tuple-element.13.refs_0_), channel_id=1, source_target_pairs={{0,32},{8,40},{16,48},{24,56},{32,64},{40,72},{48,80},{56,88},{64,... | collective-permute-start | bytes 589832 | tf_op jit(solution)/shard_map/ppermute | solution.py:302
  26.2 23.9 %collective-permute-start.3 = (bf16[2,384,128]{2,1,0:T(8,128)(2,1)}, bf16[2,384,128]{2,1,0:T(8,128)(2,1)S(1)}, u32[]{:S(2)}, u32[]{:S(2)}) collective-permute-start(bf16[2,384,128]{2,1,0:T(8,128)(2,1)} %get-tuple-element.13.refs_0_), channel_id=1, source_target_pairs={{0,16},{8,24},{16,32},{24,40},{32,48},{40,56},{48,64},{56,72},{64,... | collective-permute-start | bytes 589832 | tf_op jit(solution)/shard_map/ppermute | solution.py:302
  28.4 64.2 %collective-permute-start.2 = (bf16[8,64,512]{2,1,0:T(8,128)(2,1)S(1)}, bf16[8,64,512]{2,1,0:T(8,128)(2,1)S(1)}, u32[]{:S(2)}, u32[]{:S(2)}) collective-permute-start(bf16[8,64,512]{2,1,0:T(8,128)(2,1)S(1)} %all-to-all-done.refs_1_.own), channel_id=1, source_target_pairs={{0,384},{128,0},{256,128},{384,256},{1,385},{129,1},{257,129},{385... | collective-permute-start | bytes 1572872 | tf_op jit(solution)/shard_map/ppermute | solution.py:298
  38.1 54.5 %collective-permute-start.1 = (bf16[8,64,512]{2,1,0:T(8,128)(2,1)S(1)}, bf16[8,64,512]{2,1,0:T(8,128)(2,1)}, u32[]{:S(2)}, u32[]{:S(2)}) collective-permute-start(bf16[8,64,512]{2,1,0:T(8,128)(2,1)S(1)} %all-to-all-done.refs_1_.own), channel_id=1, source_target_pairs={{0,128},{128,256},{256,384},{384,0},{1,129},{129,257},{257,385},{3... | collective-permute-start | bytes 1572872 | tf_op jit(solution)/shard_map/ppermute | solution.py:297
  41.8 66.5 %copy-start.11 = (bf16[2,384,128]{2,1,0:T(8,128)(2,1)S(1)}, bf16[2,384,128]{2,1,0:T(8,128)(2,1)}, u32[]{:S(2)}) copy-start(bf16[2,384,128]{2,1,0:T(8,128)(2,1)} %get-tuple-element.13.refs_0_) | copy-start | bytes 589828
  41.8 66.5 %copy-start.12 = (s32[2]{0:T(128)S(1)}, s32[2]{0:T(128)}, u32[]{:S(2)}) copy-start(s32[2]{0:T(128)} %pad_add_fusion.place_ref) | copy-start | bytes 28
  41.8 66.5 %copy-start.14 = (s32[1,16]{1,0:T(1,128)S(1)}, s32[1,16]{1,0:T(1,128)}, u32[]{:S(2)}) copy-start(s32[1,16]{1,0:T(1,128)} %listed_ref.5) | copy-start | bytes 196
  41.8 66.5 %copy-start.15 = (bf16[384,512]{1,0:T(8,128)(2,1)S(1)}, bf16[384,512]{1,0:T(8,128)(2,1)}, u32[]{:S(2)}) copy-start(bf16[384,512]{1,0:T(8,128)(2,1)} %q_ref.3) | copy-start | bytes 1179652
  41.8 66.5 %copy-start.16 = (s32[1,768]{1,0:T(1,128)S(1)}, s32[1,768]{1,0:T(1,128)}, u32[]{:S(2)}) copy-start(s32[1,768]{1,0:T(1,128)} %slash_ref.1) | copy-start | bytes 9220
  41.8 50.8 %all-to-all-start.1 = ((bf16[32,32,128]{2,1,0:T(8,128)(2,1)}), bf16[32,32,128]{2,1,0:T(8,128)(2,1)S(1)}, u32[]{:S(2)}, u32[]{:S(2)}) async-start(bf16[32,32,128]{2,1,0:T(8,128)(2,1)} %after.1), calls=%async_computation.1 | async-start | bytes 524288 | tf_op jit(solution)/shard_map/all_to_all | solution.py:305
  53.6 54.7 %copy-start.4 = (bf16[2,384,128]{2,1,0:T(8,128)(2,1)S(1)}, bf16[2,384,128]{2,1,0:T(8,128)(2,1)}, u32[]{:S(2)}) copy-start(bf16[2,384,128]{2,1,0:T(8,128)(2,1)} %copy-done.3) | copy-start | bytes 589828
  53.6 54.7 %copy-start.6 = (bf16[2,384,128]{2,1,0:T(8,128)(2,1)S(1)}, bf16[2,384,128]{2,1,0:T(8,128)(2,1)}, u32[]{:S(2)}) copy-start(bf16[2,384,128]{2,1,0:T(8,128)(2,1)} %copy-done.5) | copy-start | bytes 589828
  53.6 54.7 %copy-start.8 = (bf16[2,384,128]{2,1,0:T(8,128)(2,1)S(1)}, bf16[2,384,128]{2,1,0:T(8,128)(2,1)}, u32[]{:S(2)}) copy-start(bf16[2,384,128]{2,1,0:T(8,128)(2,1)} %copy-done.7) | copy-start | bytes 589828
  53.6 54.6 %collective-permute-start.7 = (bf16[3,2,384,128]{3,2,1,0:T(8,128)(2,1)}, bf16[3,2,384,128]{3,2,1,0:T(8,128)(2,1)S(1)}, u32[]{:S(2)}, u32[]{:S(2)}) collective-permute-start(bf16[3,2,384,128]{3,2,1,0:T(8,128)(2,1)} %choose.1), channel_id=1, source_target_pairs={{0,8},{8,0},{1,9},{9,1},{2,10},{10,2},{3,11},{11,3},{4,12},{12,4},... | collective-permute-start | bytes 1769480 | tf_op jit(solution)/shard_map/ppermute | solution.py:253
  95.2 28.0 %all-to-all-start.2 = ((bf16[32,32,128]{2,1,0:T(8,128)(2,1)}), bf16[32,32,128]{2,1,0:T(8,128)(2,1)S(1)}, u32[]{:S(2)}, u32[]{:S(2)}) async-start(bf16[32,32,128]{2,1,0:T(8,128)(2,1)} %total.1), calls=%async_computation.2 | async-start | bytes 524288 | tf_op jit(solution)/shard_map/all_to_all | solution.py:310
  100.1 20.6 %collective-permute-start.9 = (bf16[4,64,512]{2,1,0:T(8,128)(2,1)S(1)}, bf16[4,64,512]{2,1,0:T(8,128)(2,1)S(1)}, u32[]{:S(2)}, u32[]{:S(2)}) collective-permute-start(bf16[4,64,512]{2,1,0:T(8,128)(2,1)S(1)} %slice.9), channel_id=1, source_target_pairs={{0,384},{128,0},{256,128},{384,256},{1,385},{129,1},{257,129},{385... | collective-permute-start | bytes 786440 | tf_op jit(solution)/shard_map/ppermute | solution.py:353
  106.4 16.9 %collective-permute-start.8 = (bf16[4,64,512]{2,1,0:T(8,128)(2,1)S(1)}, bf16[4,64,512]{2,1,0:T(8,128)(2,1)S(1)}, u32[]{:S(2)}, u32[]{:S(2)}) collective-permute-start(bf16[4,64,512]{2,1,0:T(8,128)(2,1)S(1)} %slice.8), channel_id=1, source_target_pairs={{0,128},{128,256},{256,384},{384,0},{1,129},{129,257},{257,385},{3... | collective-permute-start | bytes 786440 | tf_op jit(solution)/shard_map/ppermute | solution.py:352
  119.7 77.0 %copy-start.13 = (s32[2]{0:T(128)S(1)}, s32[2]{0:T(128)}, u32[]{:S(2)}) copy-start(s32[2]{0:T(128)} %pad_add_fusion.place_ref) | copy-start | bytes 28
  120.6 76.1 %copy-start.10 = (f32[3,512,128]{2,1,0:T(8,128)S(1)}, f32[3,512,128]{2,1,0:T(8,128)}, u32[]{:S(2)}) copy-start(f32[3,512,128]{2,1,0:T(8,128)} %copy-done.9) | copy-start | bytes 2359300
  189.4 14.8 %collective-permute-start.10 = (bf16[4,8,64,512]{3,2,1,0:T(8,128)(2,1)}, bf16[4,8,64,512]{3,2,1,0:T(8,128)(2,1)S(1)}, u32[]{:S(2)}, u32[]{:S(2)}) collective-permute-start(bf16[4,8,64,512]{3,2,1,0:T(8,128)(2,1)} %collect.1.w_mine), channel_id=1, source_target_pairs={{0,8},{8,0},{1,9},{9,1},{2,10},{10,2},{3,11},{11,3},{4,12},{12,4},... | collective-permute-start | bytes 6291464 | tf_op jit(solution)/shard_map/ppermute | solution.py:253
  192.4 4.3 %collective-permute-start.6 = (bf16[8,2,64,128]{3,2,1,0:T(8,128)(2,1)}, bf16[8,2,64,128]{3,2,1,0:T(8,128)(2,1)S(1)}, u32[]{:S(2)}, u32[]{:S(2)}) collective-permute-start(bf16[8,2,64,128]{3,2,1,0:T(8,128)(2,1)} %bitcast.7), channel_id=1, source_target_pairs={{0,8},{8,0},{1,9},{9,1},{2,10},{10,2},{3,11},{11,3},{4,12},{12,4},... | collective-permute-start | bytes 786440 | tf_op jit(solution)/shard_map/ppermute | solution.py:253
  (14 other events, 39.9 us)

commit v3 on v2

--- a/solution.py
+++ b/solution.py
@@ -26,12 +26,10 @@
     return [pl.BlockSpec(memory_space=pltpu.VMEM)] * n
 
 
-def pick_kernel(place_ref, listed_ref, k_ref, v_ref, pair_ref, keep_ref, send_ref):
+def pick_kernel(place_ref, listed_ref, k_ref, v_ref, keep_ref, send_ref):
     rows = k_ref.shape[0]
     base = place_ref[0] * (rows // BLK)
     flip = place_ref[1] * keep_ref.shape[0]
-    pair_ref[0] = k_ref[...]
-    pair_ref[1] = v_ref[...]
     half = keep_ref.shape[0]
     for slot in range(2 * half):
         block = listed_ref[0, (slot + flip) % (2 * half)] - base
@@ -43,6 +41,13 @@
             out[slot % half, part] = jnp.where(here, got, 0.0).astype(jnp.bfloat16)
 
 
+def merge_kernel(keep_ref, got_ref, k_ref, v_ref, blocks_ref, pair_ref):
+    total = keep_ref[...].astype(jnp.float32) + got_ref[...].astype(jnp.float32)
+    blocks_ref[...] = total.astype(jnp.bfloat16)
+    pair_ref[0] = k_ref[...]
+    pair_ref[1] = v_ref[...]
+
+
 def choose_kernel(place_ref, *refs):
     own, out_ref = refs[:4], refs[4]
     for core in (0, 1):
@@ -72,28 +77,10 @@
     return out
 
 
-def collect_kernel(place_ref, own, up, down, far_lo, far_hi, late, later, out_ref, sems):
-    n_zh, n_y = out_ref.shape[:2]
-    me = place_ref[0] // (2 * n_y)
-    mid = n_y // 2
-    far = out_ref.at[lax.rem(me + 2, n_zh)]
-    pieces = (
-        (own, out_ref.at[me]),
-        (up, out_ref.at[lax.rem(me + n_zh - 1, n_zh)]),
-        (down, out_ref.at[lax.rem(me + 1, n_zh)]),
-        (far_lo, far.at[:mid]),
-        (far_hi, far.at[mid:]),
-    )
-    copies = [pltpu.make_async_copy(a, b, sems.at[i]) for i, (a, b) in enumerate(pieces)]
-    for copy in copies:
-        copy.start()
-    for copy in copies:
-        copy.wait()
-
-
 def band_kernel(place_ref, listed_ref, q_ref, slash_ref, *refs):
     own, other = refs[:4], refs[4]
-    (acc_ref, top_ref, sum_ref), (diag, col, bias, kwin, vwin, s_scr) = refs[5:8], refs[8:]
+    (acc_ref, top_ref, sum_ref, token_ref), (diag, col, bias, kwin, vwin, s_scr) = refs[5:9], refs[9:]
+    token_ref[...] = jnp.zeros_like(token_ref)
     rows = q_ref.shape[0]
     span = SLASH_MAX + QB
     lead = 7 * rows - rows - SLASH_MAX
@@ -205,48 +192,43 @@
             attended[pl.ds(first, QB), h * HD : (h + 1) * HD] = out[h * QB : (h + 1) * QB]
 
 
-def project_kernel(place_ref, att_ref, w_mine, w_other, out_ref, w_scr, sem_in, out_scr, sem_out):
-    core = place_ref[1]
-    n_zh, n_y = w_mine.shape[0], w_mine.shape[1]
+def project_kernel(att_ref, w_ref, out_ref, w_scr, sem_in, out_scr, sem_out):
+    parts, span, inner = w_scr.shape
     width = 512
-    per = width // w_scr.shape[2] // 2
-    span = out_ref.shape[1] // n_zh
-
-    def fetch(z, i):
-        src, at = ((w_mine, core), (w_other, 1 - core))[i]
-        dst = w_scr.at[pl.ds(z * n_y, n_y), at]
-        return pltpu.make_async_copy(src.at[z], dst, sem_in.at[z, i])
-
-    def store(z):
+
+    def fetch(i):
+        return pltpu.make_async_copy(w_ref.at[i * span : (i + 1) * span], w_scr.at[i], sem_in.at[i])
+
+    def store(i):
         return pltpu.make_async_copy(
-            out_scr.at[z], out_ref.at[:, z * span : (z + 1) * span], sem_out.at[z]
+            out_scr.at[i], out_ref.at[:, i * span : (i + 1) * span], sem_out.at[i]
         )
 
-    for z in range(n_zh):
-        fetch(z, 0).start()
-        fetch(z, 1).start()
-    for z in range(n_zh):
-        fetch(z, 0).wait()
-        fetch(z, 1).wait()
-        for n in range(span // width):
-            w = w_scr[z * n_y + n * per : z * n_y + (n + 1) * per].reshape(width, GROUP * HD)
-            out_scr[z, :, n * width : (n + 1) * width] = lax.dot_general(
-                att_ref[...], w, NT, preferred_element_type=jnp.float32
+    for i in range(parts):
+        fetch(i).start()
+    for i in range(parts):
+        fetch(i).wait()
+        for n in range(0, span, width):
+            out_scr[i, :, n : n + width] = lax.dot_general(
+                att_ref[...], w_scr[i, n : n + width], NT, preferred_element_type=jnp.float32
             ).astype(jnp.bfloat16)
-        store(z).start()
-    for z in range(n_zh):
-        store(z).wait()
-
-
-def after(x, *others):
+        store(i).start()
+    for i in range(parts):
+        store(i).wait()
+
+
+def after_kernel(x_ref, token_ref, out_ref):
+    out_ref[...] = x_ref[...]
+
+
+def after(x, token):
     return pl.pallas_call(
-        lambda *refs: None,
-        in_specs=[pl.BlockSpec(memory_space=pl.ANY)] * (1 + len(others)),
-        out_specs=pl.BlockSpec(memory_space=pl.ANY),
+        after_kernel,
+        in_specs=vmem(2),
+        out_specs=vmem(1)[0],
         out_shape=jax.ShapeDtypeStruct(x.shape, x.dtype),
-        input_output_aliases={0: 0},
         name="after",
-    )(x, *others)
+    )(x, token)
 
 
 def swap(x):
@@ -279,36 +261,45 @@
     def shape(*dims, dtype=bf16):
         return jax.ShapeDtypeStruct(dims, dtype)
 
-    pair, keep, send = pl.pallas_call(
+    keep, send = pl.pallas_call(
         pick_kernel,
         in_specs=smem * 2 + vmem(2),
-        out_specs=vmem(3),
+        out_specs=vmem(2),
         out_shape=[
-            shape(2, rows, width),
             shape(half, 2, BLK, width),
             shape(half, 2, BLK, width),
         ],
         name="pick",
     )(where, vertical, keys, values)
 
-    up = [(i, (i + 1) % n_zh) for i in range(n_zh)]
-    down = [(i, (i - 1) % n_zh) for i in range(n_zh)]
-    w = spread(out_weight.T, "y")
-    w_up = lax.ppermute(w, "zh", up)
-    w_down = lax.ppermute(w, "zh", down)
-
-    own = [pair]
-    for k in (1, 2, 3):
-        own.append(lax.ppermute(pair, CTX, [(i, i + 2 * k) for i in range(n_ctx - 2 * k)]))
-
-    blocks = (keep + swap(send)).reshape(n_zh * n_y, -1, width)
-    parts = lax.all_to_all(after(blocks, w), ZY, 0, 0, tiled=True)
-    parts = pl.pallas_call(
-        total_kernel, in_specs=vmem(1) + hbm * 5, out_specs=vmem(1)[0],
-        out_shape=shape(*parts.shape), name="total",
-    )(parts, w_up, w_down, *own[1:])
+    blocks, pair = pl.pallas_call(
+        merge_kernel,
+        in_specs=vmem(4),
+        out_specs=vmem(2),
+        out_shape=[
+            shape(half, 2, BLK, width),
+            shape(2, rows, width),
+        ],
+        name="merge",
+    )(keep, swap(send), keys, values)
+
+    w = lax.all_gather(out_weight.T, CTX, axis=0, tiled=True)
+
+    def ahead(x, chips):
+        return lax.ppermute(x, CTX, [(i, i + 2 * chips) for i in range(n_ctx - 2 * chips)])
+
+    own = [pair] + [ahead(pair, chips) for chips in (1, 2, 3)]
+
+    def total(x, copies, *before):
+        return pl.pallas_call(
+            total_kernel, in_specs=vmem(1) + hbm * len(before), out_specs=vmem(1)[0],
+            out_shape=shape(copies, *x.shape[1:]), name="total",
+        )(x, *before)
+
+    blocks = blocks.reshape(n_zh * n_y, -1, width)
+    parts = lax.all_to_all(blocks, ZY, 0, 0, tiled=True)
+    parts = total(parts, n_zh * n_y)
     far_mine = lax.all_to_all(parts, ZY, 0, 0, tiled=True).reshape(half, 2, BLK, width)
-    far_other = swap(far_mine)
 
     other = swap(pl.pallas_call(
         choose_kernel, in_specs=smem + vmem(4), out_specs=vmem(1)[0],
@@ -317,11 +308,11 @@
 
     steps = rows // QB
     stats = shape(steps, GROUP * QB, HD, dtype=f32)
-    acc, top, total = pl.pallas_call(
+    acc, top, sums, token = pl.pallas_call(
         band_kernel,
         in_specs=smem * 2 + vmem(7),
-        out_specs=vmem(3),
-        out_shape=[stats, stats, stats],
+        out_specs=vmem(4),
+        out_shape=[stats, stats, stats, shape(8, HD, dtype=f32)],
         scratch_shapes=[
             pltpu.VMEM((QB, span), f32),
             pltpu.VMEM((1, 7 * rows), f32),
@@ -339,22 +330,7 @@
         name="band",
     )(where, vertical, query, slash, *own, other)
 
-    mid = n_y // 2
-    w_mine = pl.pallas_call(
-        collect_kernel,
-        in_specs=smem + hbm * 7,
-        out_specs=hbm[0],
-        out_shape=shape(n_zh, *w.shape),
-        scratch_shapes=[pltpu.SemaphoreType.DMA((5,))],
-        name="collect",
-    )(
-        where, w, w_up, w_down,
-        lax.ppermute(w_up[:mid], "zh", up),
-        lax.ppermute(w_down[mid:], "zh", down),
-        far_mine, acc,
-    )
-    w_other = swap(w_mine)
-
+    far_other = swap(after(far_mine, token))
     n_far = 2 * half * BLK
     attended = pl.pallas_call(
         far_kernel,
@@ -369,17 +345,17 @@
             transcendentals=rows * GROUP * n_far,
         ),
         name="far",
-    )(where, vertical, query, far_mine, far_other, acc, top, total)
+    )(where, vertical, query, far_mine, far_other, acc, top, sums)
 
     d_model = cols * n_ctx
-    partial_sum = pl.pallas_call(
+    term = pl.pallas_call(
         project_kernel,
-        in_specs=smem + vmem(1) + hbm * 2,
+        in_specs=vmem(1) + hbm,
         out_specs=hbm[0],
         out_shape=shape(rows, d_model),
         scratch_shapes=[
-            pltpu.VMEM((n_zh * n_y, 2, cols, inner), bf16),
-            pltpu.SemaphoreType.DMA((n_zh, 2)),
+            pltpu.VMEM((n_zh, d_model // n_zh, inner), bf16),
+            pltpu.SemaphoreType.DMA((n_zh,)),
             pltpu.VMEM((n_zh, rows, d_model // n_zh), bf16),
             pltpu.SemaphoreType.DMA((n_zh,)),
         ],
@@ -388,8 +364,9 @@
             flops=2 * rows * inner * d_model, bytes_accessed=8_000_000, transcendentals=0
         ),
         name="project",
-    )(where, attended, w_mine, w_other)
-    received = lax.all_to_all(partial_sum.reshape(8, rows // 8, d_model), KV, 0, 0, tiled=True)
+    )(attended, w)
+    n_kv = lax.axis_size(KV)
+    received = lax.all_to_all(term.reshape(n_kv, rows // n_kv, d_model), KV, 0, 0, tiled=True)
     return summed(received)
 
 

time: 253 us -> 185 us (0.73)
  Pallas kernels: 90.3 us -> 28.2 us
  starting transfers between devices: 68.5 us -> 47.9 us
  between operations: 0.36 us -> 13.6 us
  waiting for transfers between devices: 36.3 us -> 40.1 us
    pallas_call x6, Pallas kernels: 82.9 us -> 20.7 us  [the longest x1 9.52 us: body(): pl.pallas_call(band_kernel, in_specs=smem * 2 + vmem(7), out_specs=vmem(4...]
    ppermute x7 -> x3, starting transfers between devices: 30.7 us -> 6.69 us  [ahead(): lax.ppermute(x, CTX, [(i, i + 2 * chips) for i in range(n_ctx - 2 * chips)])]
    all_gather x0 -> x1, waiting for transfers between devices: none -> 16.6 us  [body(): w = lax.all_gather(out_weight.T, CTX, axis=0, tiled=True)]
    all_to_all x2 -> x1, waiting for transfers between devices: 30.4 us -> 18.5 us  [body(): parts = lax.all_to_all(blocks, ZY, 0, 0, tiled=True)]
    all_to_all x1, starting transfers between devices: 3.87 us -> 11.7 us  [body(): lax.all_to_all(parts, ZY, 0, 0, tiled=True).reshape(half, 2, BLK, width)]
    ppermute x4 -> x3, starting transfers between devices: 18.1 us -> 14.6 us  [swap(): return lax.ppermute(x, 'c', [(0, 1), (1, 0)])]
    unnamed x48 -> x36, local copies, waits for them, and re-layouts: 6.99 us -> 10.1 us
    all_to_all x2 -> x1, starting transfers between devices: 15.9 us -> 15 us  [body(): parts = lax.all_to_all(blocks, ZY, 0, 0, tiled=True)]
  transfers between devices with their start and end apart: 14 -> 9, of which waited for: 4 -> 5; matrix products, arithmetic and copies ran while one was open for 2% -> 0% of each run, Pallas kernels for 8% -> 13%
where the time goes in v3:
time: 185 us; the launch traced here: 184 us
  starting transfers between devices  47.9 us (26%)
  blocking collectives  42.4 us (23%)
  waiting for transfers between devices  40.1 us (22%)
  Pallas kernels  28.2 us (15%)
  between operations  13.6 us (7%)
  local copies, waits for them, and re-layouts  10.1 us (5%)
  other arithmetic  1.88 us (1%)
    all_to_all x1, blocking collectives, body(): lax.all_to_all(term.reshape(n_kv, rows // n_kv, d_model), KV, 0, 0, tiled...  42.4 us
    all_to_all x1, waiting for transfers between devices, body(): parts = lax.all_to_all(blocks, ZY, 0, 0, tiled=True)  18.5 us
    all_gather x1, waiting for transfers between devices, body(): w = lax.all_gather(out_weight.T, CTX, axis=0, tiled=True)  16.6 us
    all_to_all x1, starting transfers between devices, body(): parts = lax.all_to_all(blocks, ZY, 0, 0, tiled=True)  15 us
    ppermute x3, starting transfers between devices, swap(): return lax.ppermute(x, 'c', [(0, 1), (1, 0)])  14.6 us
    all_to_all x1, starting transfers between devices, body(): lax.all_to_all(parts, ZY, 0, 0, tiled=True).reshape(half, 2, BLK, width)  11.7 us
    unnamed x36, local copies, waits for them, and re-layouts  10.1 us
    pallas_call x1, Pallas kernels, body(): pl.pallas_call(band_kernel, in_specs=smem * 2 + vmem(7), out_specs=vmem(4...  9.52 us
  transfers between devices with their start and end apart: 9, of which 5 were waited for; matrix products, arithmetic and copies ran while one was open for 0% of the time, Pallas kernels for 13%

profile of v3, /device:TPU:1, one launch (start us, length us, event | category | flops | bytes accessed | tf_op | source)
XLA Modules:
  0.0 184.2 jit_solution(17387135333366989700)
XLA Ops:
  7.8 1.9 %pick.1 = (bf16[8,2,64,128]{3,2,1,0:T(8,128)(2,1)}, bf16[8,2,64,128]{3,2,1,0:T(8,128)(2,1)}) custom-call(s32[2]{0:T(128)} %pad_add_fusion.place_ref, s32[1,16]{1,0:T(1,128)} %listed_ref.5, bf16[384,128]{1,0:T(8,128)(2,1)} %k_ref.3, bf16[384,128]{1,0:T(8,128)(2,1)} %v_ref.3), custom_call_target="tpu_custom_call" | custom-call | tf_op jit(solution)/shard_map/pick/pallas_call | solution.py:264
  9.7 8.8 %collective-permute-start = (bf16[8,2,64,128]{3,2,1,0:T(8,128)(2,1)}, bf16[8,2,64,128]{3,2,1,0:T(8,128)(2,1)S(1)}, u32[]{:S(2)}, u32[]{:S(2)}) collective-permute-start(bf16[8,2,64,128]{3,2,1,0:T(8,128)(2,1)} %get-tuple-element.14), channel_id=1, source_target_pairs={{0,8},{8,0},{1,9},{9,1},{2,10},{10,2},{3,11},{11,3},{4,12},{12,4},... | collective-permute-start | bytes 786440 | tf_op jit(solution)/shard_map/ppermute | solution.py:235
  18.5 1.4 collective-permute-done.got_ref
  20.5 1.9 %merge.1 = (bf16[8,2,64,128]{3,2,1,0:T(8,128)(2,1)}, bf16[2,384,128]{2,1,0:T(8,128)(2,1)}) custom-call(bf16[8,2,64,128]{3,2,1,0:T(8,128)(2,1)} %get-tuple-element.13.keep_ref, bf16[8,2,64,128]{3,2,1,0:T(8,128)(2,1)} %copy-done.17, bf16[384,128]{1,0:T(8,128)(2,1)} %k_ref.3, bf16[384,128]{1,0:T(8,128)(2,1)} %v_ref.3), custom_call_target="tpu_custom_call" | custom-call | tf_op jit(solution)/shard_map/merge/pallas_call | solution.py:275
  22.4 1.3 collective-permute-start.1
  23.7 1.3 collective-permute-start.2
  25.0 4.1 %collective-permute-start.3 = (bf16[2,384,128]{2,1,0:T(8,128)(2,1)}, bf16[2,384,128]{2,1,0:T(8,128)(2,1)S(1)}, u32[]{:S(2)}, u32[]{:S(2)}) collective-permute-start(bf16[2,384,128]{2,1,0:T(8,128)(2,1)} %get-tuple-element.16.refs_0_), channel_id=1, source_target_pairs={{0,48},{8,56},{16,64},{24,72},{32,80},{40,88},{48,96},{56,104},{64... | collective-permute-start | bytes 589832 | tf_op jit(solution)/shard_map/ppermute | solution.py:289
  29.1 15.0 %all-to-all-start = ((bf16[32,32,128]{2,1,0:T(8,128)(2,1)}), bf16[32,32,128]{2,1,0:T(8,128)(2,1)S(1)}, u32[]{:S(2)}, u32[]{:S(2)}) async-start(bf16[32,32,128]{2,1,0:T(8,128)(2,1)} %bitcast.9), calls=%async_computation | async-start | bytes 524288 | tf_op jit(solution)/shard_map/all_to_all | solution.py:300
  44.2 1.6 collective-permute-done.3.refs_3_
  46.5 2.1 %choose.1 = bf16[3,2,384,128]{3,2,1,0:T(8,128)(2,1)} custom-call(s32[2]{0:T(128)} %pad_add_fusion.place_ref, bf16[2,384,128]{2,1,0:T(8,128)(2,1)} %get-tuple-element.16.refs_0_, bf16[2,384,128]{2,1,0:T(8,128)(2,1)} %copy-done.3, bf16[2,384,128]{2,1,0:T(8,128)(2,1)} %copy-done.5, bf16[2,384,128]{2,1,0:T(8,128)(2,1)} %copy-done.7), custom_call_target="tpu_custom_call" | custom-call | tf_op jit(solution)/shard_map/choose/pallas_call | solution.py:304
  48.6 3.5 %collective-permute-start.4 = (bf16[3,2,384,128]{3,2,1,0:T(8,128)(2,1)}, bf16[3,2,384,128]{3,2,1,0:T(8,128)(2,1)S(1)}, u32[]{:S(2)}, u32[]{:S(2)}) collective-permute-start(bf16[3,2,384,128]{3,2,1,0:T(8,128)(2,1)} %choose.1), channel_id=1, source_target_pairs={{0,8},{8,0},{1,9},{9,1},{2,10},{10,2},{3,11},{11,3},{4,12},{12,4},... | collective-permute-start | bytes 1769480 | tf_op jit(solution)/shard_map/ppermute | solution.py:235
  52.0 18.5 %all-to-all-done.x_ref = bf16[32,32,128]{2,1,0:T(8,128)(2,1)S(1)} async-done(((bf16[32,32,128]{2,1,0:T(8,128)(2,1)}), bf16[32,32,128]{2,1,0:T(8,128)(2,1)S(1)}, u32[]{:S(2)}, u32[]{:S(2)}) %all-to-all-start) | async-done | bytes 262176 | tf_op jit(solution)/shard_map/all_to_all | solution.py:300
  71.2 1.7 total.1
  72.9 11.7 %all-to-all-start.1 = ((bf16[32,32,128]{2,1,0:T(8,128)(2,1)}), bf16[32,32,128]{2,1,0:T(8,128)(2,1)S(1)}, u32[]{:S(2)}, u32[]{:S(2)}) async-start(bf16[32,32,128]{2,1,0:T(8,128)(2,1)} %total.1), calls=%async_computation.1 | async-start | bytes 524288 | tf_op jit(solution)/shard_map/all_to_all | solution.py:302
  88.4 9.5 %band.1 = (f32[3,512,128]{2,1,0:T(8,128)S(1)}, f32[3,512,128]{2,1,0:T(8,128)S(1)}, f32[3,512,128]{2,1,0:T(8,128)S(1)}, f32[8,128]{1,0:T(8,128)S(1)}) custom-call(s32[2]{0:T(128)S(1)} %copy-done.10, s32[1,16]{1,0:T(1,128)S(1)} %copy-done.11, bf16[384,512]{1,0:T(8,128)(2,1)S(1)} %copy-done.12, s32[1,768]{1,0:T(1,128)S(1)} %copy-done.13, ...), custom_call_target="tpu_custom_call" | custom-call | flops 3422552064 | bytes 8000000 | tf_op jit(solution)/shard_map/band/pallas_call | solution.py:311
  100.1 1.7 after.1
  101.8 2.4 %collective-permute-start.5 = (bf16[8,2,64,128]{3,2,1,0:T(8,128)(2,1)}, bf16[8,2,64,128]{3,2,1,0:T(8,128)(2,1)S(1)}, u32[]{:S(2)}, u32[]{:S(2)}) collective-permute-start(bf16[8,2,64,128]{3,2,1,0:T(8,128)(2,1)} %after.1), channel_id=1, source_target_pairs={{0,8},{8,0},{1,9},{9,1},{2,10},{10,2},{3,11},{11,3},{4,12},{12,4},... | collective-permute-start | bytes 786440 | tf_op jit(solution)/shard_map/ppermute | solution.py:235
  104.1 1.4 collective-permute-done.5.other_ref
  106.4 1.1 copy-done.15
  107.6 5.4 %far.1.att_ref = bf16[384,512]{1,0:T(8,128)(2,1)S(1)} custom-call(s32[2]{0:T(128)S(1)} %copy-done.10, s32[1,16]{1,0:T(1,128)S(1)} %copy-done.11, bf16[384,512]{1,0:T(8,128)(2,1)S(1)} %copy-done.12, bf16[8,2,64,128]{3,2,1,0:T(8,128)(2,1)S(1)} %bitcast.8, bf16[8,2,64,128]{3,2,1,0:T(8,128)(2,1)S(1)} %collective-permute-done.5.other_ref, ...), custom_call_target="tpu_custom_call" | custom-call | flops 1610612736 | bytes 8000000 | tf_op jit(solution)/shard_map/far/pallas_call | solution.py:335
  113.0 16.6 %all-gather.2.cloned.1.call-done.w_ref = bf16[4096,512]{1,0:T(8,128)(2,1)} async-done(((bf16[64,512]{1,0:T(8,128)(2,1)}), bf16[4096,512]{1,0:T(8,128)(2,1)}) %all-gather.2.cloned.1.call-update) | async-done | bytes 4194320 | tf_op jit(solution)/shard_map/all_gather | solution.py:286
  129.6 4.0 %project.1 = bf16[384,4096]{1,0:T(8,128)(2,1)S(1)} custom-call(bf16[384,512]{1,0:T(8,128)(2,1)S(1)} %far.1.att_ref, bf16[4096,512]{1,0:T(8,128)(2,1)} %all-gather.2.cloned.1.call-done.w_ref), custom_call_target="tpu_custom_call" | custom-call | flops 1610612736 | bytes 8000000 | tf_op jit(solution)/shard_map/project/pallas_call | solution.py:351
  133.6 42.4 %all_to_all.15 = bf16[8,48,4096]{2,1,0:T(8,128)(2,1)S(1)} all-to-all(bf16[8,48,4096]{2,1,0:T(8,128)(2,1)S(1)} %bitcast.6), channel_id=1, replica_groups=mesh['zh'=4,'y'=8,'c'=2,'x'=4,'zl'=2] {'x','zl'}, dimensions={0} | all-to-all | bytes 6291456 | tf_op jit(solution)/shard_map/all_to_all | solution.py:369
  176.0 1.3 reduce_sum.12
  (42 shorter events, 10.2 us)
Async XLA Ops:
  6.5 78.1 %copy-start.11 = (s32[1,16]{1,0:T(1,128)S(1)}, s32[1,16]{1,0:T(1,128)}, u32[]{:S(2)}) copy-start(s32[1,16]{1,0:T(1,128)} %listed_ref.5) | copy-start | bytes 196
  6.5 78.1 %copy-start.13 = (s32[1,768]{1,0:T(1,128)S(1)}, s32[1,768]{1,0:T(1,128)}, u32[]{:S(2)}) copy-start(s32[1,768]{1,0:T(1,128)} %slash_ref.1) | copy-start | bytes 9220
  6.5 78.1 %copy-start.12 = (bf16[384,512]{1,0:T(8,128)(2,1)S(1)}, bf16[384,512]{1,0:T(8,128)(2,1)}, u32[]{:S(2)}) copy-start(bf16[384,512]{1,0:T(8,128)(2,1)} %q_ref.3) | copy-start | bytes 1179652
  6.5 123.0 %all-gather.2.cloned.1.call-start = ((), (), s32[]{:S(2)}) async-start(), calls=%async_computation.3 | async-start | bytes 4259840 | tf_op jit(solution)/shard_map/all_gather | solution.py:286
  7.8 76.8 %copy-start.10 = (s32[2]{0:T(128)S(1)}, s32[2]{0:T(128)}, u32[]{:S(2)}) copy-start(s32[2]{0:T(128)} %pad_add_fusion.place_ref) | copy-start | bytes 28
  9.7 10.1 %collective-permute-start = (bf16[8,2,64,128]{3,2,1,0:T(8,128)(2,1)}, bf16[8,2,64,128]{3,2,1,0:T(8,128)(2,1)S(1)}, u32[]{:S(2)}, u32[]{:S(2)}) collective-permute-start(bf16[8,2,64,128]{3,2,1,0:T(8,128)(2,1)} %get-tuple-element.14), channel_id=1, source_target_pairs={{0,8},{8,0},{1,9},{9,1},{2,10},{10,2},{3,11},{11,3},{4,12},{12,4},... | collective-permute-start | bytes 786440 | tf_op jit(solution)/shard_map/ppermute | solution.py:235
  22.4 21.7 %collective-permute-start.1 = (bf16[2,384,128]{2,1,0:T(8,128)(2,1)}, bf16[2,384,128]{2,1,0:T(8,128)(2,1)S(1)}, u32[]{:S(2)}, u32[]{:S(2)}) collective-permute-start(bf16[2,384,128]{2,1,0:T(8,128)(2,1)} %get-tuple-element.16.refs_0_), channel_id=1, source_target_pairs={{0,16},{8,24},{16,32},{24,40},{32,48},{40,56},{48,64},{56,72},{64,... | collective-permute-start | bytes 589832 | tf_op jit(solution)/shard_map/ppermute | solution.py:289
  23.7 20.4 %collective-permute-start.2 = (bf16[2,384,128]{2,1,0:T(8,128)(2,1)}, bf16[2,384,128]{2,1,0:T(8,128)(2,1)S(1)}, u32[]{:S(2)}, u32[]{:S(2)}) collective-permute-start(bf16[2,384,128]{2,1,0:T(8,128)(2,1)} %get-tuple-element.16.refs_0_), channel_id=1, source_target_pairs={{0,32},{8,40},{16,48},{24,56},{32,64},{40,72},{48,80},{56,88},{64,... | collective-permute-start | bytes 589832 | tf_op jit(solution)/shard_map/ppermute | solution.py:289
  25.0 20.7 %collective-permute-start.3 = (bf16[2,384,128]{2,1,0:T(8,128)(2,1)}, bf16[2,384,128]{2,1,0:T(8,128)(2,1)S(1)}, u32[]{:S(2)}, u32[]{:S(2)}) collective-permute-start(bf16[2,384,128]{2,1,0:T(8,128)(2,1)} %get-tuple-element.16.refs_0_), channel_id=1, source_target_pairs={{0,48},{8,56},{16,64},{24,72},{32,80},{40,88},{48,96},{56,104},{64... | collective-permute-start | bytes 589832 | tf_op jit(solution)/shard_map/ppermute | solution.py:289
  29.1 41.4 %all-to-all-start = ((bf16[32,32,128]{2,1,0:T(8,128)(2,1)}), bf16[32,32,128]{2,1,0:T(8,128)(2,1)S(1)}, u32[]{:S(2)}, u32[]{:S(2)}) async-start(bf16[32,32,128]{2,1,0:T(8,128)(2,1)} %bitcast.9), calls=%async_computation | async-start | bytes 524288 | tf_op jit(solution)/shard_map/all_to_all | solution.py:300
  44.2 1.6 copy-start.3
  44.2 1.6 copy-start.5
  48.6 36.0 %collective-permute-start.4 = (bf16[3,2,384,128]{3,2,1,0:T(8,128)(2,1)}, bf16[3,2,384,128]{3,2,1,0:T(8,128)(2,1)S(1)}, u32[]{:S(2)}, u32[]{:S(2)}) collective-permute-start(bf16[3,2,384,128]{3,2,1,0:T(8,128)(2,1)} %choose.1), channel_id=1, source_target_pairs={{0,8},{8,0},{1,9},{9,1},{2,10},{10,2},{3,11},{11,3},{4,12},{12,4},... | collective-permute-start | bytes 1769480 | tf_op jit(solution)/shard_map/ppermute | solution.py:235
  70.5 0.7 copy-start.16
  72.9 26.5 %all-to-all-start.1 = ((bf16[32,32,128]{2,1,0:T(8,128)(2,1)}), bf16[32,32,128]{2,1,0:T(8,128)(2,1)S(1)}, u32[]{:S(2)}, u32[]{:S(2)}) async-start(bf16[32,32,128]{2,1,0:T(8,128)(2,1)} %total.1), calls=%async_computation.1 | async-start | bytes 524288 | tf_op jit(solution)/shard_map/all_to_all | solution.py:302
  84.6 0.9 copy-start.2
  85.6 0.9 copy-start.4
  86.5 0.9 copy-start.6
  87.4 0.9 copy-start.8
  98.5 0.9 copy-start.14
  99.4 0.7 copy-start
  101.8 3.7 %collective-permute-start.5 = (bf16[8,2,64,128]{3,2,1,0:T(8,128)(2,1)}, bf16[8,2,64,128]{3,2,1,0:T(8,128)(2,1)S(1)}, u32[]{:S(2)}, u32[]{:S(2)}) collective-permute-start(bf16[8,2,64,128]{3,2,1,0:T(8,128)(2,1)} %after.1), channel_id=1, source_target_pairs={{0,8},{8,0},{1,9},{9,1},{2,10},{10,2},{3,11},{11,3},{4,12},{12,4},... | collective-permute-start | bytes 786440 | tf_op jit(solution)/shard_map/ppermute | solution.py:235
  105.5 0.9 copy-start.1
  106.4 1.1 copy-start.15
  (3 other events, 2.0 us)
Sparse Core Ops, SparseCore 0:
  10.7 118.7 all-gather.1

commit v4 on v3

--- a/solution.py
+++ b/solution.py
@@ -19,33 +19,43 @@
 ZY = ("zh", "y")
 SCALE = math.log2(math.e) / math.sqrt(HD)
 NT = (((1,), (1,)), ((), ()))
-VMEM_LIMIT = 48 * 1024 * 1024
+MIB = 1024 * 1024
+SMALL = pltpu.CompilerParams(vmem_limit_bytes=6 * MIB)
 
 
 def vmem(n):
     return [pl.BlockSpec(memory_space=pltpu.VMEM)] * n
 
 
-def pick_kernel(place_ref, listed_ref, k_ref, v_ref, keep_ref, send_ref):
-    rows = k_ref.shape[0]
-    base = place_ref[0] * (rows // BLK)
-    flip = place_ref[1] * keep_ref.shape[0]
-    half = keep_ref.shape[0]
-    for slot in range(2 * half):
-        block = listed_ref[0, (slot + flip) % (2 * half)] - base
-        here = jnp.logical_and(block >= 0, block < rows // BLK)
-        row = pl.multiple_of(jnp.clip(block, 0, rows // BLK - 1) * BLK, BLK)
-        out = keep_ref if slot < half else send_ref
-        for part, ref in enumerate((k_ref, v_ref)):
-            got = ref[pl.ds(row, BLK), :].astype(jnp.float32)
-            out[slot % half, part] = jnp.where(here, got, 0.0).astype(jnp.bfloat16)
-
-
-def merge_kernel(keep_ref, got_ref, k_ref, v_ref, blocks_ref, pair_ref):
-    total = keep_ref[...].astype(jnp.float32) + got_ref[...].astype(jnp.float32)
-    blocks_ref[...] = total.astype(jnp.bfloat16)
+def pack_kernel(k_ref, v_ref, w_ref, pair_ref, pack_ref):
+    rows, width = k_ref.shape
     pair_ref[0] = k_ref[...]
     pair_ref[1] = v_ref[...]
+    pack_ref[:rows] = k_ref[...]
+    pack_ref[rows : 2 * rows] = v_ref[...]
+    cols = w_ref.shape[0]
+    for i in range(w_ref.shape[1] // width):
+        at = 2 * rows + i * cols
+        pack_ref[at : at + cols] = w_ref[:, i * width : (i + 1) * width]
+
+
+def pick_kernel(place_ref, listed_ref, pack_ref, ready_ref, out_ref, w_ref):
+    n_dev, n_row, _ = pack_ref.shape
+    rows = (n_row - w_ref.shape[1]) // 2
+    per_shard = rows // BLK
+    half = out_ref.shape[0]
+    core = place_ref[1]
+    for slot in range(half):
+        block = listed_ref[0, slot + core * half]
+        holder = lax.div(block, per_shard)
+        here = lax.div(lax.rem(holder, place_ref[3]), 2) == place_ref[2]
+        row = pl.multiple_of(lax.rem(block, per_shard) * BLK, BLK)
+        dev = 2 * lax.div(holder, place_ref[3]) + lax.rem(holder, 2)
+        for part in range(2):
+            got = pack_ref[dev, pl.ds(part * rows + row, BLK), :].astype(jnp.float32)
+            out_ref[slot, part] = jnp.where(here, got, 0.0).astype(jnp.bfloat16)
+    for zh in range(n_dev // 2):
+        w_ref[zh] = pack_ref[2 * zh + core, 2 * rows :]
 
 
 def choose_kernel(place_ref, *refs):
@@ -57,8 +67,7 @@
                 out_ref[k] = own[k + core][...]
 
 
-def total_kernel(x_ref, *refs):
-    out_ref = refs[-1]
+def total_kernel(x_ref, ready_ref, out_ref):
     total = jnp.sum(x_ref[...].astype(jnp.float32), axis=0).astype(jnp.bfloat16)
     for i in range(out_ref.shape[0]):
         out_ref[i] = total
@@ -193,42 +202,34 @@
 
 
 def project_kernel(att_ref, w_ref, out_ref, w_scr, sem_in, out_scr, sem_out):
-    parts, span, inner = w_scr.shape
-    width = 512
-
-    def fetch(i):
-        return pltpu.make_async_copy(w_ref.at[i * span : (i + 1) * span], w_scr.at[i], sem_in.at[i])
-
-    def store(i):
+    n_y, n_core, n_zh, group, cols, width = w_ref.shape
+    span = out_ref.shape[1] // n_zh
+    step = 512
+    per = step // (n_core * cols)
+
+    def fetch(z, h):
+        dst = w_scr.at[z, :, :, :, pl.ds(h * width, width)]
+        return pltpu.make_async_copy(w_ref.at[:, :, z, h], dst, sem_in.at[z, h])
+
+    def store(z):
         return pltpu.make_async_copy(
-            out_scr.at[i], out_ref.at[:, i * span : (i + 1) * span], sem_out.at[i]
+            out_scr.at[z], out_ref.at[:, z * span : (z + 1) * span], sem_out.at[z]
         )
 
-    for i in range(parts):
-        fetch(i).start()
-    for i in range(parts):
-        fetch(i).wait()
-        for n in range(0, span, width):
-            out_scr[i, :, n : n + width] = lax.dot_general(
-                att_ref[...], w_scr[i, n : n + width], NT, preferred_element_type=jnp.float32
+    for z in range(n_zh):
+        for h in range(group):
+            fetch(z, h).start()
+    for z in range(n_zh):
+        for h in range(group):
+            fetch(z, h).wait()
+        for n in range(span // step):
+            w = w_scr[z, n * per : (n + 1) * per].reshape(step, group * width)
+            out_scr[z, :, n * step : (n + 1) * step] = lax.dot_general(
+                att_ref[...], w, NT, preferred_element_type=jnp.float32
             ).astype(jnp.bfloat16)
-        store(i).start()
-    for i in range(parts):
-        store(i).wait()
-
-
-def after_kernel(x_ref, token_ref, out_ref):
-    out_ref[...] = x_ref[...]
-
-
-def after(x, token):
-    return pl.pallas_call(
-        after_kernel,
-        in_specs=vmem(2),
-        out_specs=vmem(1)[0],
-        out_shape=jax.ShapeDtypeStruct(x.shape, x.dtype),
-        name="after",
-    )(x, token)
+        store(z).start()
+    for z in range(n_zh):
+        store(z).wait()
 
 
 def swap(x):
@@ -256,55 +257,43 @@
     bf16, f32 = jnp.bfloat16, jnp.float32
     smem = [pl.BlockSpec(memory_space=pltpu.SMEM)]
     hbm = [pl.BlockSpec(memory_space=pl.ANY)]
-    where = jnp.stack([place, core]).astype(jnp.int32)
+    per_zh = n_y * lax.axis_size("c")
+    where = jnp.stack([place, core, lax.axis_index("y"), per_zh]).astype(jnp.int32)
 
     def shape(*dims, dtype=bf16):
         return jax.ShapeDtypeStruct(dims, dtype)
 
-    keep, send = pl.pallas_call(
+    pair, pack = pl.pallas_call(
+        pack_kernel,
+        in_specs=vmem(3),
+        out_specs=vmem(2),
+        out_shape=[shape(2, rows, width), shape(2 * rows + cols * GROUP, width)],
+        compiler_params=SMALL,
+        name="pack",
+    )(keys, values, out_weight.T)
+    pack = lax.all_gather(pack, ("zh", "c"), axis=0, tiled=False)
+
+    own = [pair]
+    for k in (1, 2, 3):
+        own.append(lax.ppermute(pair, CTX, [(i, i + 2 * k) for i in range(n_ctx - 2 * k)]))
+    other = swap(pl.pallas_call(
+        choose_kernel, in_specs=smem + vmem(4), out_specs=vmem(1)[0],
+        out_shape=shape(3, 2, rows, width), compiler_params=SMALL, name="choose",
+    )(where, *own))
+
+    blocks, wt = pl.pallas_call(
         pick_kernel,
         in_specs=smem * 2 + vmem(2),
         out_specs=vmem(2),
         out_shape=[
             shape(half, 2, BLK, width),
-            shape(half, 2, BLK, width),
+            shape(n_zh, cols * GROUP, width),
         ],
+        compiler_params=SMALL,
         name="pick",
-    )(where, vertical, keys, values)
-
-    blocks, pair = pl.pallas_call(
-        merge_kernel,
-        in_specs=vmem(4),
-        out_specs=vmem(2),
-        out_shape=[
-            shape(half, 2, BLK, width),
-            shape(2, rows, width),
-        ],
-        name="merge",
-    )(keep, swap(send), keys, values)
-
-    w = lax.all_gather(out_weight.T, CTX, axis=0, tiled=True)
-
-    def ahead(x, chips):
-        return lax.ppermute(x, CTX, [(i, i + 2 * chips) for i in range(n_ctx - 2 * chips)])
-
-    own = [pair] + [ahead(pair, chips) for chips in (1, 2, 3)]
-
-    def total(x, copies, *before):
-        return pl.pallas_call(
-            total_kernel, in_specs=vmem(1) + hbm * len(before), out_specs=vmem(1)[0],
-            out_shape=shape(copies, *x.shape[1:]), name="total",
-        )(x, *before)
-
-    blocks = blocks.reshape(n_zh * n_y, -1, width)
-    parts = lax.all_to_all(blocks, ZY, 0, 0, tiled=True)
-    parts = total(parts, n_zh * n_y)
-    far_mine = lax.all_to_all(parts, ZY, 0, 0, tiled=True).reshape(half, 2, BLK, width)
-
-    other = swap(pl.pallas_call(
-        choose_kernel, in_specs=smem + vmem(4), out_specs=vmem(1)[0],
-        out_shape=shape(3, 2, rows, width), name="choose",
-    )(where, *own))
+    )(where, vertical, pack, other)
+    w = lax.all_gather(wt, ("y", "c"), axis=0, tiled=False)
+    w = w.reshape(n_y, 2, n_zh, GROUP, cols, width)
 
     steps = rows // QB
     stats = shape(steps, GROUP * QB, HD, dtype=f32)
@@ -321,7 +310,7 @@
             pltpu.VMEM((7 * rows, HD), bf16),
             pltpu.VMEM((GROUP * QB, span), f32),
         ],
-        compiler_params=pltpu.CompilerParams(vmem_limit_bytes=VMEM_LIMIT),
+        compiler_params=pltpu.CompilerParams(vmem_limit_bytes=20 * MIB),
         cost_estimate=pl.CostEstimate(
             flops=8 * rows * GROUP * HD * span,
             bytes_accessed=8_000_000,
@@ -330,7 +319,14 @@
         name="band",
     )(where, vertical, query, slash, *own, other)
 
-    far_other = swap(after(far_mine, token))
+
+    parts = lax.all_to_all(blocks, "y", 0, 0, tiled=True)
+    parts = pl.pallas_call(
+        total_kernel, in_specs=vmem(2), out_specs=vmem(1)[0],
+        out_shape=shape(*parts.shape), compiler_params=SMALL, name="total",
+    )(parts, token)
+    far_mine = lax.all_to_all(parts, "y", 0, 0, tiled=True)
+    far_other = swap(far_mine)
     n_far = 2 * half * BLK
     attended = pl.pallas_call(
         far_kernel,
@@ -338,7 +334,7 @@
         out_specs=vmem(1)[0],
         out_shape=shape(rows, GROUP * HD),
         scratch_shapes=[pltpu.VMEM((n_far, HD), bf16), pltpu.VMEM((n_far, HD), bf16)],
-        compiler_params=pltpu.CompilerParams(vmem_limit_bytes=VMEM_LIMIT),
+        compiler_params=pltpu.CompilerParams(vmem_limit_bytes=20 * MIB),
         cost_estimate=pl.CostEstimate(
             flops=8 * rows * GROUP * HD * n_far,
             bytes_accessed=8_000_000,
@@ -354,12 +350,12 @@
         out_specs=hbm[0],
         out_shape=shape(rows, d_model),
         scratch_shapes=[
-            pltpu.VMEM((n_zh, d_model // n_zh, inner), bf16),
-            pltpu.SemaphoreType.DMA((n_zh,)),
+            pltpu.VMEM((n_zh, n_y, 2, cols, inner), bf16),
+            pltpu.SemaphoreType.DMA((n_zh, GROUP)),
             pltpu.VMEM((n_zh, rows, d_model // n_zh), bf16),
             pltpu.SemaphoreType.DMA((n_zh,)),
         ],
-        compiler_params=pltpu.CompilerParams(vmem_limit_bytes=VMEM_LIMIT),
+        compiler_params=pltpu.CompilerParams(vmem_limit_bytes=48 * MIB),
         cost_estimate=pl.CostEstimate(
             flops=2 * rows * inner * d_model, bytes_accessed=8_000_000, transcendentals=0
         ),

time: 185 us -> 178 us (0.962)
  starting transfers between devices: 47.9 us -> 27.6 us
  blocking collectives: 42.4 us -> 61 us
  Pallas kernels: 28.2 us -> 21.9 us
  waiting for transfers between devices: 40.1 us -> 43.1 us
    all_to_all x2 -> x1, starting transfers between devices: 26.7 us -> 5.26 us  [body(): parts = lax.all_to_all(blocks, 'y', 0, 0, tiled=True)]
    all_to_all x0 -> x1, blocking collectives: none -> 20.5 us  [body(): far_mine = lax.all_to_all(parts, 'y', 0, 0, tiled=True)]
    all_to_all x2 -> x1, waiting for transfers between devices: 18.5 us -> 0.79 us  [body(): parts = lax.all_to_all(blocks, 'y', 0, 0, tiled=True)]
    all_gather x1 -> x2, waiting for transfers between devices: 16.6 us -> 28.8 us  [the longest x1 28.7 us: body(): pack = lax.all_gather(pack, ('zh', 'c'), axis=0, tiled=False)]
    ppermute x3, waiting for transfers between devices: 1.58 us -> 10.7 us  [body(): lax.ppermute(pair, CTX, [(i, i + 2 * k) for i in range(n_ctx - 2 * k)])]
    ppermute x3, starting transfers between devices: 6.69 us -> 12.9 us  [body(): lax.ppermute(pair, CTX, [(i, i + 2 * k) for i in range(n_ctx - 2 * k)])]
    ppermute x3 -> x2, starting transfers between devices: 14.6 us -> 9.35 us  [swap(): return lax.ppermute(x, 'c', [(0, 1), (1, 0)])]
    pallas_call x3 -> x2, Pallas kernels: 5.31 us -> 0.8 us  [the longest x1 0.76 us: body(): pl.pallas_call(pack_kernel, in_specs=vmem(3), out_specs=vmem(2), out_shap...]
  transfers between devices with their start and end apart: 9 -> 8, of which waited for: 5 -> 5; matrix products, arithmetic and copies ran while one was open for 0% -> 0% of each run, Pallas kernels for 13% -> 9%
where the time goes in v4:
time: 178 us; the launch traced here: 177 us
  blocking collectives  61 us (34%)
  waiting for transfers between devices  43.1 us (24%)
  starting transfers between devices  27.6 us (16%)
  Pallas kernels  21.9 us (12%)
  between operations  13.5 us (8%)
  local copies, waits for them, and re-layouts  8.96 us (5%)
    all_to_all x1, blocking collectives, body(): lax.all_to_all(term.reshape(n_kv, rows // n_kv, d_model), KV, 0, 0, tiled...  40.5 us
    all_gather x1, waiting for transfers between devices, body(): pack = lax.all_gather(pack, ('zh', 'c'), axis=0, tiled=False)  28.7 us
    all_to_all x1, blocking collectives, body(): far_mine = lax.all_to_all(parts, 'y', 0, 0, tiled=True)  20.5 us
    ppermute x3, starting transfers between devices, body(): lax.ppermute(pair, CTX, [(i, i + 2 * k) for i in range(n_ctx - 2 * k)])  12.9 us
    ppermute x3, waiting for transfers between devices, body(): lax.ppermute(pair, CTX, [(i, i + 2 * k) for i in range(n_ctx - 2 * k)])  10.7 us
    pallas_call x1, Pallas kernels, body(): pl.pallas_call(band_kernel, in_specs=smem * 2 + vmem(7), out_specs=vmem(4...  9.59 us
    ppermute x2, starting transfers between devices, swap(): return lax.ppermute(x, 'c', [(0, 1), (1, 0)])  9.35 us
    unnamed x24, local copies, waits for them, and re-layouts  8.96 us
  transfers between devices with their start and end apart: 8, of which 5 were waited for; matrix products, arithmetic and copies ran while one was open for 0% of the time, Pallas kernels for 9%

profile of v4, /device:TPU:1, one launch (start us, length us, event | category | flops | bytes accessed | tf_op | source)
XLA Modules:
  0.0 177.4 jit_solution(4314019218936963529)
XLA Ops:
  6.5 0.9 copy-done.1
  7.4 0.9 copy-done.2
  10.0 4.0 %collective-permute-start = (bf16[2,384,128]{2,1,0:T(8,128)(2,1)S(1)}, bf16[2,384,128]{2,1,0:T(8,128)(2,1)S(1)}, u32[]{:S(2)}, u32[]{:S(2)}) collective-permute-start(bf16[2,384,128]{2,1,0:T(8,128)(2,1)S(1)} %get-tuple-element.14.refs_0_), channel_id=1, source_target_pairs={{0,16},{8,24},{16,32},{24,40},{32,48},{40,56},{48,64},{56,72},{64,... | collective-permute-start | bytes 589832 | tf_op jit(solution)/shard_map/ppermute | solution.py:278
  14.1 4.2 %collective-permute-start.1 = (bf16[2,384,128]{2,1,0:T(8,128)(2,1)S(1)}, bf16[2,384,128]{2,1,0:T(8,128)(2,1)S(1)}, u32[]{:S(2)}, u32[]{:S(2)}) collective-permute-start(bf16[2,384,128]{2,1,0:T(8,128)(2,1)S(1)} %get-tuple-element.14.refs_0_), channel_id=1, source_target_pairs={{0,32},{8,40},{16,48},{24,56},{32,64},{40,72},{48,80},{56,88},{64,... | collective-permute-start | bytes 589832 | tf_op jit(solution)/shard_map/ppermute | solution.py:278
  18.3 4.6 %collective-permute-start.2 = (bf16[2,384,128]{2,1,0:T(8,128)(2,1)S(1)}, bf16[2,384,128]{2,1,0:T(8,128)(2,1)S(1)}, u32[]{:S(2)}, u32[]{:S(2)}) collective-permute-start(bf16[2,384,128]{2,1,0:T(8,128)(2,1)S(1)} %get-tuple-element.14.refs_0_), channel_id=1, source_target_pairs={{0,48},{8,56},{16,64},{24,72},{32,80},{40,88},{48,96},{56,104},{64... | collective-permute-start | bytes 589832 | tf_op jit(solution)/shard_map/ppermute | solution.py:278
  23.0 10.7 %collective-permute-done.2.refs_3_ = bf16[2,384,128]{2,1,0:T(8,128)(2,1)S(1)} collective-permute-done((bf16[2,384,128]{2,1,0:T(8,128)(2,1)S(1)}, bf16[2,384,128]{2,1,0:T(8,128)(2,1)S(1)}, u32[]{:S(2)}, u32[]{:S(2)}) %collective-permute-start.2) | collective-permute-done | bytes 196640 | tf_op jit(solution)/shard_map/ppermute | solution.py:278
  34.4 6.2 %collective-permute-start.3 = (bf16[3,2,384,128]{3,2,1,0:T(8,128)(2,1)S(1)}, bf16[3,2,384,128]{3,2,1,0:T(8,128)(2,1)S(1)}, u32[]{:S(2)}, u32[]{:S(2)}) collective-permute-start(bf16[3,2,384,128]{3,2,1,0:T(8,128)(2,1)S(1)} %choose.1), channel_id=1, source_target_pairs={{0,8},{8,0},{1,9},{9,1},{2,10},{10,2},{3,11},{11,3},{4,12},{12,4},... | collective-permute-start | bytes 1769480 | tf_op jit(solution)/shard_map/ppermute | solution.py:236
  40.6 1.6 collective-permute-done.3.ready_ref.refs_4_
  42.2 28.7 %all-gather.5.cloned.1.call-done = bf16[8192,128]{1,0:T(8,128)(2,1)} async-done(((bf16[1024,128]{1,0:T(8,128)(2,1)}), bf16[8192,128]{1,0:T(8,128)(2,1)}) %all-gather.5.cloned.1.call-update) | async-done | bytes 2097168 | tf_op jit(solution)/shard_map/all_gather | solution.py:274
  70.9 1.6 copy-done
  73.2 1.4 pick.1
  74.6 5.3 %all-to-all-start = ((bf16[8,2,64,128]{3,2,1,0:T(8,128)(2,1)}), bf16[8,2,64,128]{3,2,1,0:T(8,128)(2,1)S(1)}, u32[]{:S(2)}, u32[]{:S(2)}) async-start(bf16[8,2,64,128]{3,2,1,0:T(8,128)(2,1)} %get-tuple-element.15), calls=%async_computation | async-start | bytes 524288 | tf_op jit(solution)/shard_map/all_to_all | solution.py:323
  79.9 9.6 %band.1 = (f32[3,512,128]{2,1,0:T(8,128)S(1)}, f32[3,512,128]{2,1,0:T(8,128)S(1)}, f32[3,512,128]{2,1,0:T(8,128)S(1)}, f32[8,128]{1,0:T(8,128)S(1)}) custom-call(s32[4]{0:T(128)S(1)} %pad_add_fusion.place_ref, s32[1,16]{1,0:T(1,128)S(1)} %copy-done.5, bf16[384,512]{1,0:T(8,128)(2,1)S(1)} %copy-done.6, s32[1,768]{1,0:T(1,128)S(1)} %copy-done.7, ...), custom_call_target="tpu_custom_call" | custom-call | flops 3422552064 | bytes 8000000 | tf_op jit(solution)/shard_map/band/pallas_call | solution.py:300
  89.5 0.9 copy-done.8
  90.4 0.9 copy-done.10
  92.1 20.5 %all_to_all.15.mine_ref = bf16[8,2,64,128]{3,2,1,0:T(8,128)(2,1)S(1)} all-to-all(bf16[8,2,64,128]{3,2,1,0:T(8,128)(2,1)S(1)} %total.1), channel_id=1, replica_groups=mesh['zh'=4,'y'=8,'c'=2,'x'=4,'zl'=2] {'y'}, dimensions={0} | all-to-all | bytes 524288 | tf_op jit(solution)/shard_map/all_to_all | solution.py:328
  112.6 3.1 %collective-permute-start.4 = (bf16[8,2,64,128]{3,2,1,0:T(8,128)(2,1)S(1)}, bf16[8,2,64,128]{3,2,1,0:T(8,128)(2,1)S(1)}, u32[]{:S(2)}, u32[]{:S(2)}) collective-permute-start(bf16[8,2,64,128]{3,2,1,0:T(8,128)(2,1)S(1)} %all_to_all.15.mine_ref), channel_id=1, source_target_pairs={{0,8},{8,0},{1,9},{9,1},{2,10},{10,2},{3,11},{11,3},{4,12},{12,4},... | collective-permute-start | bytes 786440 | tf_op jit(solution)/shard_map/ppermute | solution.py:236
  115.8 1.2 collective-permute-done.4.other_ref
  117.0 1.1 copy-done.9
  118.1 1.1 copy-done.11
  119.2 5.3 %far.1.att_ref = bf16[384,512]{1,0:T(8,128)(2,1)S(1)} custom-call(s32[4]{0:T(128)S(1)} %pad_add_fusion.place_ref, s32[1,16]{1,0:T(1,128)S(1)} %copy-done.5, bf16[384,512]{1,0:T(8,128)(2,1)S(1)} %copy-done.6, bf16[8,2,64,128]{3,2,1,0:T(8,128)(2,1)S(1)} %all_to_all.15.mine_ref, bf16[8,2,64,128]{3,2,1,0:T(8,128)(2,1)S(1)} %collective-permute-done.4.other_ref, ...), custom_call_target="tpu_custom_call" | custom-call | flops 1610612736 | bytes 8000000 | tf_op jit(solution)/shard_map/far/pallas_call | solution.py:331
  124.6 4.1 %project.1 = bf16[384,4096]{1,0:T(8,128)(2,1)S(1)} custom-call(bf16[384,512]{1,0:T(8,128)(2,1)S(1)} %far.1.att_ref, bf16[8,2,4,4,64,128]{5,4,3,2,1,0:T(8,128)(2,1)} %bitcast.10), custom_call_target="tpu_custom_call" | custom-call | flops 1610612736 | bytes 8000000 | tf_op jit(solution)/shard_map/project/pallas_call | solution.py:347
  128.7 40.5 %all_to_all.16 = bf16[8,48,4096]{2,1,0:T(8,128)(2,1)S(1)} all-to-all(bf16[8,48,4096]{2,1,0:T(8,128)(2,1)S(1)} %bitcast.7), channel_id=1, replica_groups=mesh['zh'=4,'y'=8,'c'=2,'x'=4,'zl'=2] {'x','zl'}, dimensions={0} | all-to-all | bytes 6291456 | tf_op jit(solution)/shard_map/all_to_all | solution.py:365
  169.3 1.3 reduce_sum.12
  (29 shorter events, 3.9 us)
Async XLA Ops:
  6.5 73.3 %copy-start.5 = (s32[1,16]{1,0:T(1,128)S(1)}, s32[1,16]{1,0:T(1,128)}, u32[]{:S(2)}) copy-start(s32[1,16]{1,0:T(1,128)} %listed_ref.5) | copy-start | bytes 196
  6.5 64.4 %all-gather.5.cloned.1.call-start = ((), (), s32[]{:S(2)}) async-start(), calls=%async_computation.3 | async-start | bytes 2359296 | tf_op jit(solution)/shard_map/all_gather | solution.py:274
  6.5 0.9 copy-start.1
  7.4 0.9 copy-start.2
  8.3 0.8 copy-start.3
  9.2 70.7 %copy-start.6 = (bf16[384,512]{1,0:T(8,128)(2,1)S(1)}, bf16[384,512]{1,0:T(8,128)(2,1)}, u32[]{:S(2)}) copy-start(bf16[384,512]{1,0:T(8,128)(2,1)} %q_ref.3) | copy-start | bytes 1179652
  9.2 70.7 %copy-start.7 = (s32[1,768]{1,0:T(1,128)S(1)}, s32[1,768]{1,0:T(1,128)}, u32[]{:S(2)}) copy-start(s32[1,768]{1,0:T(1,128)} %slash_ref.1) | copy-start | bytes 9220
  10.0 114.6 %all-gather.7.cloned.1.call-start = ((), (), s32[]{:S(2)}) async-start(), calls=%async_computation.4 | async-start | bytes 4456448 | tf_op jit(solution)/shard_map/all_gather | solution.py:295
  10.0 13.0 %collective-permute-start = (bf16[2,384,128]{2,1,0:T(8,128)(2,1)S(1)}, bf16[2,384,128]{2,1,0:T(8,128)(2,1)S(1)}, u32[]{:S(2)}, u32[]{:S(2)}) collective-permute-start(bf16[2,384,128]{2,1,0:T(8,128)(2,1)S(1)} %get-tuple-element.14.refs_0_), channel_id=1, source_target_pairs={{0,16},{8,24},{16,32},{24,40},{32,48},{40,56},{48,64},{56,72},{64,... | collective-permute-start | bytes 589832 | tf_op jit(solution)/shard_map/ppermute | solution.py:278
  14.1 9.0 %collective-permute-start.1 = (bf16[2,384,128]{2,1,0:T(8,128)(2,1)S(1)}, bf16[2,384,128]{2,1,0:T(8,128)(2,1)S(1)}, u32[]{:S(2)}, u32[]{:S(2)}) collective-permute-start(bf16[2,384,128]{2,1,0:T(8,128)(2,1)S(1)} %get-tuple-element.14.refs_0_), channel_id=1, source_target_pairs={{0,32},{8,40},{16,48},{24,56},{32,64},{40,72},{48,80},{56,88},{64,... | collective-permute-start | bytes 589832 | tf_op jit(solution)/shard_map/ppermute | solution.py:278
  18.3 15.5 %collective-permute-start.2 = (bf16[2,384,128]{2,1,0:T(8,128)(2,1)S(1)}, bf16[2,384,128]{2,1,0:T(8,128)(2,1)S(1)}, u32[]{:S(2)}, u32[]{:S(2)}) collective-permute-start(bf16[2,384,128]{2,1,0:T(8,128)(2,1)S(1)} %get-tuple-element.14.refs_0_), channel_id=1, source_target_pairs={{0,48},{8,56},{16,64},{24,72},{32,80},{40,88},{48,96},{56,104},{64... | collective-permute-start | bytes 589832 | tf_op jit(solution)/shard_map/ppermute | solution.py:278
  34.4 7.8 %collective-permute-start.3 = (bf16[3,2,384,128]{3,2,1,0:T(8,128)(2,1)S(1)}, bf16[3,2,384,128]{3,2,1,0:T(8,128)(2,1)S(1)}, u32[]{:S(2)}, u32[]{:S(2)}) collective-permute-start(bf16[3,2,384,128]{3,2,1,0:T(8,128)(2,1)S(1)} %choose.1), channel_id=1, source_target_pairs={{0,8},{8,0},{1,9},{9,1},{2,10},{10,2},{3,11},{11,3},{4,12},{12,4},... | collective-permute-start | bytes 1769480 | tf_op jit(solution)/shard_map/ppermute | solution.py:236
  70.9 1.6 copy-start
  72.5 0.7 copy-start.4
  74.6 17.5 %all-to-all-start = ((bf16[8,2,64,128]{3,2,1,0:T(8,128)(2,1)}), bf16[8,2,64,128]{3,2,1,0:T(8,128)(2,1)S(1)}, u32[]{:S(2)}, u32[]{:S(2)}) async-start(bf16[8,2,64,128]{3,2,1,0:T(8,128)(2,1)} %get-tuple-element.15), calls=%async_computation | async-start | bytes 524288 | tf_op jit(solution)/shard_map/all_to_all | solution.py:323
  89.5 0.9 copy-start.8
  90.4 0.9 copy-start.10
  112.6 4.3 %collective-permute-start.4 = (bf16[8,2,64,128]{3,2,1,0:T(8,128)(2,1)S(1)}, bf16[8,2,64,128]{3,2,1,0:T(8,128)(2,1)S(1)}, u32[]{:S(2)}, u32[]{:S(2)}) collective-permute-start(bf16[8,2,64,128]{3,2,1,0:T(8,128)(2,1)S(1)} %all_to_all.15.mine_ref), channel_id=1, source_target_pairs={{0,8},{8,0},{1,9},{9,1},{2,10},{10,2},{3,11},{11,3},{4,12},{12,4},... | collective-permute-start | bytes 786440 | tf_op jit(solution)/shard_map/ppermute | solution.py:236
  117.0 1.2 copy-start.9
  118.1 1.1 copy-start.11
Sparse Core Ops, SparseCore 0:
  10.1 60.7 all-gather.4
  74.7 46.4 all-gather.6

commit v5 on v4

--- a/solution.py
+++ b/solution.py
@@ -96,7 +96,8 @@
     for i in range(7):
         piece = own[3 - i // 2] if i % 2 == 0 else other.at[2 - i // 2]
         kwin[i * rows : (i + 1) * rows] = piece[0]
-        vwin[i * rows : (i + 1) * rows] = piece[1]
+        vwin[i * rows : (i + 1) * rows, :HD] = piece[1]
+    vwin[:, HD:] = jnp.ones((7 * rows, HD), jnp.bfloat16)
 
     at = SLASH_MAX - slash_ref[...]
     n_off = at.shape[1]
@@ -138,15 +139,13 @@
             top = jnp.maximum(top, lane_fold(jnp.maximum, s))
         top = jnp.max(top, axis=1, keepdims=True)
         shift = top * SCALE
-        acc = jnp.zeros((GROUP * QB, HD), jnp.float32)
-        total = jnp.zeros((GROUP * QB, HD), jnp.float32)
+        acc = jnp.zeros((GROUP * QB, 2 * HD), jnp.float32)
         for at, width in chunks:
             p = jnp.exp2(s_scr[:, at : at + width] * SCALE - shift)
-            total = total + lane_fold(jnp.add, p)
             v = vwin[pl.ds(base + at, width), :]
             acc = acc + jnp.dot(p.astype(jnp.bfloat16), v, preferred_element_type=jnp.float32)
-        acc_ref[step] = acc
-        sum_ref[step] = total
+        acc_ref[step] = acc[:, :HD]
+        sum_ref[step] = acc[:, HD:]
         top_ref[step] = jnp.broadcast_to(top, (GROUP * QB, HD))
 
 
@@ -159,8 +158,9 @@
         for j, ref in enumerate((mine_ref, other_ref)):
             at = (j * half + i) * BLK
             kfar[at : at + BLK] = ref[i, 0]
-            vfar[at : at + BLK] = ref[i, 1]
+            vfar[at : at + BLK, :HD] = ref[i, 1]
     n_far = kfar.shape[0]
+    vfar[:, HD:] = jnp.ones((n_far, HD), jnp.bfloat16)
     chunks = [(at, 256) for at in range(0, n_far, 256)]
     lane = lax.broadcasted_iota(jnp.int32, (1, 256), 1)
     positions = []
@@ -188,15 +188,14 @@
         top = jnp.max(top, axis=1, keepdims=True)
         shift = top * SCALE
         fade = jnp.exp2(band_top * SCALE - shift)
-        acc = acc_ref[step] * fade
-        total = sum_ref[step] * fade
+        acc = jnp.zeros((GROUP * QB, 2 * HD), jnp.float32)
         for (at, width), s in zip(chunks, scores):
             p = jnp.exp2(s * SCALE - shift)
-            total = total + lane_fold(jnp.add, p)
             acc = acc + jnp.dot(
                 p.astype(jnp.bfloat16), vfar[at : at + width], preferred_element_type=jnp.float32
             )
-        out = (acc / jnp.sum(total, axis=1, keepdims=True)).astype(jnp.bfloat16)
+        total = sum_ref[step] * fade + acc[:, HD:]
+        out = ((acc_ref[step] * fade + acc[:, :HD]) / total).astype(jnp.bfloat16)
         for h in range(GROUP):
             attended[pl.ds(first, QB), h * HD : (h + 1) * HD] = out[h * QB : (h + 1) * QB]
 
@@ -307,7 +306,7 @@
             pltpu.VMEM((1, 7 * rows), f32),
             pltpu.VMEM((QB, span), f32),
             pltpu.VMEM((7 * rows, HD), bf16),
-            pltpu.VMEM((7 * rows, HD), bf16),
+            pltpu.VMEM((7 * rows, 2 * HD), bf16),
             pltpu.VMEM((GROUP * QB, span), f32),
         ],
         compiler_params=pltpu.CompilerParams(vmem_limit_bytes=20 * MIB),
@@ -333,7 +332,7 @@
         in_specs=smem * 2 + vmem(6),
         out_specs=vmem(1)[0],
         out_shape=shape(rows, GROUP * HD),
-        scratch_shapes=[pltpu.VMEM((n_far, HD), bf16), pltpu.VMEM((n_far, HD), bf16)],
+        scratch_shapes=[pltpu.VMEM((n_far, HD), bf16), pltpu.VMEM((n_far, 2 * HD), bf16)],
         compiler_params=pltpu.CompilerParams(vmem_limit_bytes=20 * MIB),
         cost_estimate=pl.CostEstimate(
             flops=8 * rows * GROUP * HD * n_far,

time: 178 us -> 178 us (level)
  no operation moved by 1% of the time
where the time goes in v5:
time: 178 us; the launch traced here: 177 us
  blocking collectives  60.5 us (34%)
  waiting for transfers between devices  42.8 us (24%)
  starting transfers between devices  28.4 us (16%)
  Pallas kernels  21.5 us (12%)
  between operations  13.5 us (8%)
  local copies, waits for them, and re-layouts  8.94 us (5%)
    all_to_all x1, blocking collectives, body(): lax.all_to_all(term.reshape(n_kv, rows // n_kv, d_model), KV, 0, 0, tiled...  40.6 us
    all_gather x1, waiting for transfers between devices, body(): pack = lax.all_gather(pack, ('zh', 'c'), axis=0, tiled=False)  28.7 us
    all_to_all x1, blocking collectives, body(): far_mine = lax.all_to_all(parts, 'y', 0, 0, tiled=True)  19.9 us
    ppermute x3, starting transfers between devices, body(): lax.ppermute(pair, CTX, [(i, i + 2 * k) for i in range(n_ctx - 2 * k)])  12.9 us
    ppermute x3, waiting for transfers between devices, body(): lax.ppermute(pair, CTX, [(i, i + 2 * k) for i in range(n_ctx - 2 * k)])  10.7 us
    ppermute x2, starting transfers between devices, swap(): return lax.ppermute(x, 'c', [(0, 1), (1, 0)])  10.2 us
    pallas_call x1, Pallas kernels, body(): pl.pallas_call(band_kernel, in_specs=smem * 2 + vmem(7), out_specs=vmem(4...  9.87 us
    unnamed x24, local copies, waits for them, and re-layouts  8.94 us
  transfers between devices with their start and end apart: 8, of which 5 were waited for; matrix products, arithmetic and copies ran while one was open for 0% of the time, Pallas kernels for 9%

profile of v5, /device:TPU:1, one launch (start us, length us, event | category | flops | bytes accessed | tf_op | source)
XLA Modules:
  0.0 177.1 jit_solution(8085774338643885100)
XLA Ops:
  6.5 0.9 copy-done.1
  7.4 0.9 copy-done.2
  10.0 4.0 %collective-permute-start = (bf16[2,384,128]{2,1,0:T(8,128)(2,1)S(1)}, bf16[2,384,128]{2,1,0:T(8,128)(2,1)S(1)}, u32[]{:S(2)}, u32[]{:S(2)}) collective-permute-start(bf16[2,384,128]{2,1,0:T(8,128)(2,1)S(1)} %get-tuple-element.14.refs_0_), channel_id=1, source_target_pairs={{0,16},{8,24},{16,32},{24,40},{32,48},{40,56},{48,64},{56,72},{64,... | collective-permute-start | bytes 589832 | tf_op jit(solution)/shard_map/ppermute | solution.py:277
  14.1 4.2 %collective-permute-start.1 = (bf16[2,384,128]{2,1,0:T(8,128)(2,1)S(1)}, bf16[2,384,128]{2,1,0:T(8,128)(2,1)S(1)}, u32[]{:S(2)}, u32[]{:S(2)}) collective-permute-start(bf16[2,384,128]{2,1,0:T(8,128)(2,1)S(1)} %get-tuple-element.14.refs_0_), channel_id=1, source_target_pairs={{0,32},{8,40},{16,48},{24,56},{32,64},{40,72},{48,80},{56,88},{64,... | collective-permute-start | bytes 589832 | tf_op jit(solution)/shard_map/ppermute | solution.py:277
  18.3 4.6 %collective-permute-start.2 = (bf16[2,384,128]{2,1,0:T(8,128)(2,1)S(1)}, bf16[2,384,128]{2,1,0:T(8,128)(2,1)S(1)}, u32[]{:S(2)}, u32[]{:S(2)}) collective-permute-start(bf16[2,384,128]{2,1,0:T(8,128)(2,1)S(1)} %get-tuple-element.14.refs_0_), channel_id=1, source_target_pairs={{0,48},{8,56},{16,64},{24,72},{32,80},{40,88},{48,96},{56,104},{64... | collective-permute-start | bytes 589832 | tf_op jit(solution)/shard_map/ppermute | solution.py:277
  23.0 10.7 %collective-permute-done.2.refs_3_ = bf16[2,384,128]{2,1,0:T(8,128)(2,1)S(1)} collective-permute-done((bf16[2,384,128]{2,1,0:T(8,128)(2,1)S(1)}, bf16[2,384,128]{2,1,0:T(8,128)(2,1)S(1)}, u32[]{:S(2)}, u32[]{:S(2)}) %collective-permute-start.2) | collective-permute-done | bytes 196640 | tf_op jit(solution)/shard_map/ppermute | solution.py:277
  34.4 6.2 %collective-permute-start.3 = (bf16[3,2,384,128]{3,2,1,0:T(8,128)(2,1)S(1)}, bf16[3,2,384,128]{3,2,1,0:T(8,128)(2,1)S(1)}, u32[]{:S(2)}, u32[]{:S(2)}) collective-permute-start(bf16[3,2,384,128]{3,2,1,0:T(8,128)(2,1)S(1)} %choose.1), channel_id=1, source_target_pairs={{0,8},{8,0},{1,9},{9,1},{2,10},{10,2},{3,11},{11,3},{4,12},{12,4},... | collective-permute-start | bytes 1769480 | tf_op jit(solution)/shard_map/ppermute | solution.py:235
  40.6 1.6 collective-permute-done.3.ready_ref.refs_4_
  42.2 28.7 %all-gather.5.cloned.1.call-done = bf16[8192,128]{1,0:T(8,128)(2,1)} async-done(((bf16[1024,128]{1,0:T(8,128)(2,1)}), bf16[8192,128]{1,0:T(8,128)(2,1)}) %all-gather.5.cloned.1.call-update) | async-done | bytes 2097168 | tf_op jit(solution)/shard_map/all_gather | solution.py:273
  70.9 1.6 copy-done
  73.2 1.4 pick.1
  74.6 5.3 %all-to-all-start = ((bf16[8,2,64,128]{3,2,1,0:T(8,128)(2,1)}), bf16[8,2,64,128]{3,2,1,0:T(8,128)(2,1)S(1)}, u32[]{:S(2)}, u32[]{:S(2)}) async-start(bf16[8,2,64,128]{3,2,1,0:T(8,128)(2,1)} %get-tuple-element.15), calls=%async_computation | async-start | bytes 524288 | tf_op jit(solution)/shard_map/all_to_all | solution.py:322
  79.9 9.9 %band.1 = (f32[3,512,128]{2,1,0:T(8,128)S(1)}, f32[3,512,128]{2,1,0:T(8,128)S(1)}, f32[3,512,128]{2,1,0:T(8,128)S(1)}, f32[8,128]{1,0:T(8,128)S(1)}) custom-call(s32[4]{0:T(128)S(1)} %pad_add_fusion.place_ref, s32[1,16]{1,0:T(1,128)S(1)} %copy-done.5, bf16[384,512]{1,0:T(8,128)(2,1)S(1)} %copy-done.6, s32[1,768]{1,0:T(1,128)S(1)} %copy-done.7, ...), custom_call_target="tpu_custom_call" | custom-call | flops 3422552064 | bytes 8000000 | tf_op jit(solution)/shard_map/band/pallas_call | solution.py:299
  89.8 0.9 copy-done.8
  90.7 0.9 copy-done.10
  92.1 19.9 %all_to_all.15.mine_ref = bf16[8,2,64,128]{3,2,1,0:T(8,128)(2,1)S(1)} all-to-all(bf16[8,2,64,128]{3,2,1,0:T(8,128)(2,1)S(1)} %total.1), channel_id=1, replica_groups=mesh['zh'=4,'y'=8,'c'=2,'x'=4,'zl'=2] {'y'}, dimensions={0} | all-to-all | bytes 524288 | tf_op jit(solution)/shard_map/all_to_all | solution.py:327
  112.0 4.0 %collective-permute-start.4 = (bf16[8,2,64,128]{3,2,1,0:T(8,128)(2,1)S(1)}, bf16[8,2,64,128]{3,2,1,0:T(8,128)(2,1)S(1)}, u32[]{:S(2)}, u32[]{:S(2)}) collective-permute-start(bf16[8,2,64,128]{3,2,1,0:T(8,128)(2,1)S(1)} %all_to_all.15.mine_ref), channel_id=1, source_target_pairs={{0,8},{8,0},{1,9},{9,1},{2,10},{10,2},{3,11},{11,3},{4,12},{12,4},... | collective-permute-start | bytes 786440 | tf_op jit(solution)/shard_map/ppermute | solution.py:235
  116.1 1.2 collective-permute-done.4.other_ref
  117.3 1.1 copy-done.9
  118.4 1.1 copy-done.11
  119.5 4.7 %far.1.att_ref = bf16[384,512]{1,0:T(8,128)(2,1)S(1)} custom-call(s32[4]{0:T(128)S(1)} %pad_add_fusion.place_ref, s32[1,16]{1,0:T(1,128)S(1)} %copy-done.5, bf16[384,512]{1,0:T(8,128)(2,1)S(1)} %copy-done.6, bf16[8,2,64,128]{3,2,1,0:T(8,128)(2,1)S(1)} %all_to_all.15.mine_ref, bf16[8,2,64,128]{3,2,1,0:T(8,128)(2,1)S(1)} %collective-permute-done.4.other_ref, ...), custom_call_target="tpu_custom_call" | custom-call | flops 1610612736 | bytes 8000000 | tf_op jit(solution)/shard_map/far/pallas_call | solution.py:330
  124.3 4.1 %project.1 = bf16[384,4096]{1,0:T(8,128)(2,1)S(1)} custom-call(bf16[384,512]{1,0:T(8,128)(2,1)S(1)} %far.1.att_ref, bf16[8,2,4,4,64,128]{5,4,3,2,1,0:T(8,128)(2,1)} %bitcast.10), custom_call_target="tpu_custom_call" | custom-call | flops 1610612736 | bytes 8000000 | tf_op jit(solution)/shard_map/project/pallas_call | solution.py:346
  128.4 40.6 %all_to_all.16 = bf16[8,48,4096]{2,1,0:T(8,128)(2,1)S(1)} all-to-all(bf16[8,48,4096]{2,1,0:T(8,128)(2,1)S(1)} %bitcast.7), channel_id=1, replica_groups=mesh['zh'=4,'y'=8,'c'=2,'x'=4,'zl'=2] {'x','zl'}, dimensions={0} | all-to-all | bytes 6291456 | tf_op jit(solution)/shard_map/all_to_all | solution.py:364
  168.9 1.3 reduce_sum.12
  (29 shorter events, 3.6 us)
Async XLA Ops:
  6.5 73.3 %copy-start.5 = (s32[1,16]{1,0:T(1,128)S(1)}, s32[1,16]{1,0:T(1,128)}, u32[]{:S(2)}) copy-start(s32[1,16]{1,0:T(1,128)} %listed_ref.5) | copy-start | bytes 196
  6.5 64.4 %all-gather.5.cloned.1.call-start = ((), (), s32[]{:S(2)}) async-start(), calls=%async_computation.3 | async-start | bytes 2359296 | tf_op jit(solution)/shard_map/all_gather | solution.py:273
  6.5 0.9 copy-start.1
  7.4 0.9 copy-start.2
  8.3 0.8 copy-start.3
  9.2 70.7 %copy-start.6 = (bf16[384,512]{1,0:T(8,128)(2,1)S(1)}, bf16[384,512]{1,0:T(8,128)(2,1)}, u32[]{:S(2)}) copy-start(bf16[384,512]{1,0:T(8,128)(2,1)} %q_ref.3) | copy-start | bytes 1179652
  9.2 70.7 %copy-start.7 = (s32[1,768]{1,0:T(1,128)S(1)}, s32[1,768]{1,0:T(1,128)}, u32[]{:S(2)}) copy-start(s32[1,768]{1,0:T(1,128)} %slash_ref.1) | copy-start | bytes 9220
  10.0 114.3 %all-gather.7.cloned.1.call-start = ((), (), s32[]{:S(2)}) async-start(), calls=%async_computation.4 | async-start | bytes 4456448 | tf_op jit(solution)/shard_map/all_gather | solution.py:294
  10.0 13.0 %collective-permute-start = (bf16[2,384,128]{2,1,0:T(8,128)(2,1)S(1)}, bf16[2,384,128]{2,1,0:T(8,128)(2,1)S(1)}, u32[]{:S(2)}, u32[]{:S(2)}) collective-permute-start(bf16[2,384,128]{2,1,0:T(8,128)(2,1)S(1)} %get-tuple-element.14.refs_0_), channel_id=1, source_target_pairs={{0,16},{8,24},{16,32},{24,40},{32,48},{40,56},{48,64},{56,72},{64,... | collective-permute-start | bytes 589832 | tf_op jit(solution)/shard_map/ppermute | solution.py:277
  14.1 9.0 %collective-permute-start.1 = (bf16[2,384,128]{2,1,0:T(8,128)(2,1)S(1)}, bf16[2,384,128]{2,1,0:T(8,128)(2,1)S(1)}, u32[]{:S(2)}, u32[]{:S(2)}) collective-permute-start(bf16[2,384,128]{2,1,0:T(8,128)(2,1)S(1)} %get-tuple-element.14.refs_0_), channel_id=1, source_target_pairs={{0,32},{8,40},{16,48},{24,56},{32,64},{40,72},{48,80},{56,88},{64,... | collective-permute-start | bytes 589832 | tf_op jit(solution)/shard_map/ppermute | solution.py:277
  18.3 15.5 %collective-permute-start.2 = (bf16[2,384,128]{2,1,0:T(8,128)(2,1)S(1)}, bf16[2,384,128]{2,1,0:T(8,128)(2,1)S(1)}, u32[]{:S(2)}, u32[]{:S(2)}) collective-permute-start(bf16[2,384,128]{2,1,0:T(8,128)(2,1)S(1)} %get-tuple-element.14.refs_0_), channel_id=1, source_target_pairs={{0,48},{8,56},{16,64},{24,72},{32,80},{40,88},{48,96},{56,104},{64... | collective-permute-start | bytes 589832 | tf_op jit(solution)/shard_map/ppermute | solution.py:277
  34.4 7.8 %collective-permute-start.3 = (bf16[3,2,384,128]{3,2,1,0:T(8,128)(2,1)S(1)}, bf16[3,2,384,128]{3,2,1,0:T(8,128)(2,1)S(1)}, u32[]{:S(2)}, u32[]{:S(2)}) collective-permute-start(bf16[3,2,384,128]{3,2,1,0:T(8,128)(2,1)S(1)} %choose.1), channel_id=1, source_target_pairs={{0,8},{8,0},{1,9},{9,1},{2,10},{10,2},{3,11},{11,3},{4,12},{12,4},... | collective-permute-start | bytes 1769480 | tf_op jit(solution)/shard_map/ppermute | solution.py:235
  70.9 1.6 copy-start
  72.5 0.7 copy-start.4
  74.6 17.5 %all-to-all-start = ((bf16[8,2,64,128]{3,2,1,0:T(8,128)(2,1)}), bf16[8,2,64,128]{3,2,1,0:T(8,128)(2,1)S(1)}, u32[]{:S(2)}, u32[]{:S(2)}) async-start(bf16[8,2,64,128]{3,2,1,0:T(8,128)(2,1)} %get-tuple-element.15), calls=%async_computation | async-start | bytes 524288 | tf_op jit(solution)/shard_map/all_to_all | solution.py:322
  89.8 0.9 copy-start.8
  90.7 0.9 copy-start.10
  112.0 5.2 %collective-permute-start.4 = (bf16[8,2,64,128]{3,2,1,0:T(8,128)(2,1)S(1)}, bf16[8,2,64,128]{3,2,1,0:T(8,128)(2,1)S(1)}, u32[]{:S(2)}, u32[]{:S(2)}) collective-permute-start(bf16[8,2,64,128]{3,2,1,0:T(8,128)(2,1)S(1)} %all_to_all.15.mine_ref), channel_id=1, source_target_pairs={{0,8},{8,0},{1,9},{9,1},{2,10},{10,2},{3,11},{11,3},{4,12},{12,4},... | collective-permute-start | bytes 786440 | tf_op jit(solution)/shard_map/ppermute | solution.py:235
  117.3 1.1 copy-start.9
  118.4 1.1 copy-start.11
Sparse Core Ops, SparseCore 0:
  10.1 60.7 all-gather.4
  74.7 46.7 all-gather.6
